TPU v7x, 1024 devices: a whole 4x8x16 slice. The times are simulated.
1024 devices in a mesh: replica: 64 (over z_lo, y), tensor: 16 (over z_hi, x, core).
Axes of the slice: x: 4, y: 8, z: 16 (z_hi: 2, z_lo: 8; z = z_hi * 8 + z_lo), core: 2. Of those that a mesh axis runs over, the one named last changes fastest.
Arguments:
- hidden: bfloat16 [64, 256, 8192], P('replica', None, 'tensor'), may hold values from -6 to 6
- key_cotangent: bfloat16 [64, 256, 512], P('replica', 'tensor'), may hold values from -1.125 to 1.125
- key_weight: bfloat16 [64, 8192, 512], P('replica', 'tensor'), may hold values from -3 to 3
- first_moment: bfloat16 [64, 8192, 512], P('replica', 'tensor'), may hold values from -1.796875 to 1.796875
- second_moment: bfloat16 [64, 8192, 512], P('replica', 'tensor'), may hold values from 0.5 to 8
- local_fragment: bfloat16 [64, 1024, 512], P('replica', 'tensor'), may hold values from -6 to 6
- global_fragment: float32 [1024, 512], P('tensor'), may hold values from -6 to 6
- outer_momentum: float32 [1024, 512], P('tensor'), may hold values from -3 to 3
Outputs:
- new_weight: bfloat16 [64, 8192, 512], P('replica', 'tensor')
- new_first: bfloat16 [64, 8192, 512], P('replica', 'tensor')
- new_second: bfloat16 [64, 8192, 512], P('replica', 'tensor')
- new_global: float32 [1024, 512], P('tensor')
- new_momentum: float32 [1024, 512], P('tensor')
All inputs are finite; a program needn't handle non-finite values.
Results may differ from a plain program's by a relative error of at most 0.001.
Values may be sent and summed in bfloat16 or wider, within the bound.
A program may use at most 32 MiB of HBM per device.

v0:
```python
import jax
import jax.numpy as jnp
from jax import lax
from jax.sharding import PartitionSpec as P

ADAM_STEP = 4


beta_one = 0.9
beta_two = 0.95
adam_eps = 1e-08
inner_rate = 0.01
decay_rate = 0.1
outer_rate = 0.7
outer_mu = 0.9


def nesterov(glob, moment, delta):
    fresh_moment = outer_mu * moment + delta
    fresh_glob = glob - outer_rate * (delta + outer_mu * fresh_moment)
    return (fresh_glob, fresh_moment)


def per_device(
    hidden,
    key_cotangent,
    key_weight,
    first_moment,
    second_moment,
    local_fragment,
    global_fragment,
    outer_momentum,
):
    acts = hidden[0]
    weight = key_weight[0]
    grad = lax.dot_general(
        acts,
        lax.all_gather(key_cotangent[0], "tensor", axis=0, tiled=True),
        (((0,), (0,)), ((), ())),
        preferred_element_type=jnp.float32,
    )
    first32 = beta_one * first_moment[0].astype(jnp.float32) + (1.0 - beta_one) * grad
    second32 = beta_two * second_moment[0].astype(jnp.float32) + (1.0 - beta_two) * grad * grad
    corr_one = 1.0 - beta_one**ADAM_STEP
    corr_two = 1.0 - beta_two**ADAM_STEP
    wfloat = weight.astype(jnp.float32)
    update = first32 / corr_one / (jnp.sqrt(second32 / corr_two) + adam_eps) + decay_rate * wfloat
    new_weight = (wfloat - inner_rate * update).astype(jnp.bfloat16)[None]
    new_first = first32.astype(jnp.bfloat16)[None]
    new_second = second32.astype(jnp.bfloat16)[None]
    replicas = lax.axis_size("replica")
    difference = global_fragment - local_fragment[0].astype(jnp.float32)
    summed = lax.psum(difference, "replica")
    new_global, new_momentum = nesterov(global_fragment, outer_momentum, summed / replicas)
    return (new_weight, new_first, new_second, new_global, new_momentum)


def solution(mesh):
    return jax.shard_map(
        per_device,
        mesh=mesh,
        in_specs=(
            P("replica", None, "tensor"),
            P("replica", "tensor", None),
            P("replica", "tensor", None),
            P("replica", "tensor", None),
            P("replica", "tensor", None),
            P("replica", "tensor", None),
            P("tensor", None),
            P("tensor", None),
        ),
        out_specs=(
            P("replica", "tensor", None),
            P("replica", "tensor", None),
            P("replica", "tensor", None),
            P("tensor", None),
            P("tensor", None),
        ),
        check_vma=False,
    )
```

profile of v0, /device:TPU:4, one launch (start us, length us, event | category | flops | bytes accessed | tf_op | source)
XLA Modules:
  0.0 833.0 jit_solution(16956390296235789450)
XLA Ops:
  7.2 0.0 copy-start
  7.2 0.0 all-reduce.2.cloned.1.call-start
  7.2 1.6 convert_subtract_fusion.1
  8.8 0.0 copy-start.3
  8.8 0.0 all-reduce.2.cloned.1.call-update
  8.9 0.7 copy-done.3
  9.6 41.9 %all-gather = bf16[1,256,512]{2,1,0:T(8,128)(2,1)S(1)} all-gather(bf16[1,16,512]{2,1,0:T(8,128)(2,1)S(1)} %copy-done.3), channel_id=2, replica_groups=mesh['replica'=64,'tensor'=16] {'tensor'}, dimensions={1}, use_global_device_ids=true | all-gather | bytes 278528 | tf_op jit(solution)/shard_map/all_gather | solution.py:38
  51.5 0.0 copy-done
  51.5 0.0 copy-start.1
  51.5 0.0 copy-start.2
  51.5 3.7 fusion.6
  55.1 769.4 %all-reduce.2.cloned.1.call-done = f32[64,512]{1,0:T(8,128)} async-done(((f32[64,512]{1,0:T(8,128)}), f32[64,512]{1,0:T(8,128)}) %all-reduce.2.cloned.1.call-update) | async-done | bytes 131088 | tf_op jit(solution)/shard_map/psum | solution.py:53
  824.5 0.0 copy-done.1
  824.5 0.0 copy-done.2
  824.5 1.6 multiply_subtract_fusion
Async XLA Ops:
  7.2 44.3 %copy-start = (bf16[1,256,512]{2,1,0:T(8,128)(2,1)S(1)}, bf16[1,256,512]{2,1,0:T(8,128)(2,1)}, u32[]{:S(2)}) copy-start(bf16[1,256,512]{2,1,0:T(8,128)(2,1)} %param.8) | copy-start | bytes 786436
  7.2 817.4 %all-reduce.2.cloned.1.call-start = ((), (), s32[]{:S(2)}) async-start(), calls=%async_computation | async-start | bytes 262144 | tf_op jit(solution)/shard_map/psum | solution.py:53
  8.8 0.7 copy-start.3
  51.5 773.1 %copy-start.1 = (f32[64,512]{1,0:T(8,128)S(1)}, f32[64,512]{1,0:T(8,128)}, u32[]{:S(2)}) copy-start(f32[64,512]{1,0:T(8,128)} %param.14) | copy-start | bytes 393220
  51.5 773.1 %copy-start.2 = (f32[64,512]{1,0:T(8,128)S(1)}, f32[64,512]{1,0:T(8,128)}, u32[]{:S(2)}) copy-start(f32[64,512]{1,0:T(8,128)} %param.15) | copy-start | bytes 393220
Sparse Core Ops, SparseCore 0:
  12.1 812.4 all-reduce.1
where the time goes:
time: 833 us
  waiting for transfers between devices  769 us (92%)
  blocking collectives  41.9 us (5%)
  between operations  14 us (2%)
    psum x1, waiting for transfers between devices, per_device(): summed = lax.psum(difference, 'replica')  769 us
    all_gather x1, blocking collectives, per_device(): lax.all_gather(key_cotangent[0], 'tensor', axis=0, tiled=True)  41.9 us
  transfers between devices with their start and end apart: 1, of which 1 were waited for; matrix products, arithmetic and copies ran while one was open for 0% of the time, Pallas kernels for 0%

commit v1 on v0

v1 whole, which is shorter than its diff:
```python
import jax
import jax.numpy as jnp
from jax import lax
from jax.experimental import pallas as pl
from jax.experimental.pallas import tpu as pltpu
from jax.sharding import PartitionSpec as P

ADAM_STEP = 4
beta_one = 0.9
beta_two = 0.95
adam_eps = 1e-08
inner_rate = 0.01
decay_rate = 0.1
outer_rate = 0.7
outer_mu = 0.9
corr_one = 1.0 - beta_one**ADAM_STEP
corr_two = 1.0 - beta_two**ADAM_STEP

MESH = pl.DeviceIdType.MESH
NY, NZ, NX, NH, NC = 8, 8, 4, 2, 2
F32 = jnp.float32
BF16 = jnp.bfloat16


def kernel(
    h_hbm, k_hbm, w_hbm, m_hbm, v_hbm, l_hbm, g_hbm, o_hbm,
    nw_ref, nm_ref, nv_ref, ng_ref, no_ref,
    h, w, m, v, g, o, cot, yb, part, zb, zg, yg,
    load_sem, send_c, recv_c, send_f, recv_f,
):
    rep, ten = lax.axis_index("replica"), lax.axis_index("tensor")
    zl, y = rep // NY, lax.rem(rep, NY)
    zh, x, c = ten // (NX * NC), lax.rem(ten // NC, NX), lax.rem(ten, NC)

    def at_y(k):
        return (zl * NY + lax.rem(y + k, NY), ten)

    def at_z(k):
        return (lax.rem(zl + k, NZ) * NY + y, ten)

    def at_x(k):
        return (rep, zh * NX * NC + lax.rem(x + k, NX) * NC + c)

    at_h = (rep, (1 - zh) * NX * NC + x * NC + c)
    at_c = (rep, zh * NX * NC + x * NC + 1 - c)

    barrier = pltpu.get_barrier_semaphore()
    partners = [at_y(k) for k in range(1, NY)] + [at_z(k) for k in range(1, NZ)] + [at_x(k) for k in range(1, NX)] + [at_h, at_c]
    for partner in partners:
        pl.semaphore_signal(barrier, inc=1, device_id=partner, device_id_type=MESH)

    def chunk(k):
        yy = lax.rem(y + k, NY)
        return l_hbm.at[pl.ds(pl.multiple_of((yy // 2) * 16, 16), 16), pl.ds(pl.multiple_of(lax.rem(yy, 2) * 256, 256), 256)]

    loads = [
        pltpu.make_async_copy(src, dst, load_sem.at[i])
        for i, (src, dst) in enumerate(
            [
                (chunk(0), yb.at[y]),
                (k_hbm, cot.at[c, zh, x]),
                (h_hbm, h),
                (w_hbm, w),
                (m_hbm, m),
                (v_hbm, v),
                (g_hbm, g),
                (o_hbm, o),
            ]
        )
    ]
    for copy in loads:
        copy.start()
    pl.semaphore_wait(barrier, len(partners))

    started = []

    def send(src, dst, sems, i, device):
        copy = pltpu.make_async_remote_copy(
            src_ref=src, dst_ref=dst, send_sem=sems[0].at[i], recv_sem=sems[1].at[i], device_id=device, device_id_type=MESH
        )
        copy.start()
        started.append(copy)
        return copy

    sc, sf = (send_c, recv_c), (send_f, recv_f)
    mine = cot.at[c, zh, x]
    theirs = cot.at[c, 1 - zh, x]
    c_h = send(k_hbm, mine, sc, 0, at_h)
    f_y = [send(chunk(k), yb.at[y], sf, k - 1, at_y(k)) for k in range(1, NY)]
    c_x = [send(k_hbm, mine, sc, k, at_x(k)) for k in range(1, NX)]

    loads[0].wait()
    for copy in f_y:
        copy.wait_recv()
    total = yb[0].astype(F32)
    for i in range(1, NY):
        total += yb[i].astype(F32)
    for i in range(NZ):
        r, q, s = i // 4, (i // 2) % 2, i % 2
        part[i] = total[r * 8 + s * 4 : r * 8 + s * 4 + 4, q * 128 : q * 128 + 128]
    f_z = [send(part.at[lax.rem(zl + k, NZ)], zb.at[zl], sf, 7 + k - 1, at_z(k)) for k in range(1, NZ)]

    c_h.wait_recv()
    c_hx = [send(theirs, theirs, sc, 3 + k, at_x(k)) for k in range(1, NX)]

    loads[1].wait()
    for copy in c_x:
        copy.wait_recv()
    row = cot.at[c, zh]
    c_c = send(row, row, sc, 7, at_c)

    for copy in f_z:
        copy.wait_recv()
    zb[zl] = part[zl]
    total = zb[0]
    for i in range(1, NZ):
        total += zb[i]
    zg[zl] = total
    f_zg = [send(zg.at[zl], zg.at[zl], sf, 14 + k - 1, at_z(k)) for k in range(1, NZ)]

    for copy in c_hx:
        copy.wait_recv()
    row = cot.at[c, 1 - zh]
    c_hc = send(row, row, sc, 8, at_c)

    for copy in f_zg:
        copy.wait_recv()
    f_yg = [send(zg, yg.at[y], sf, 21 + k - 1, at_y(k)) for k in range(1, NY)]
    for i in range(NZ):
        yg[y, i] = zg[i]

    for copy in loads[2:6]:
        copy.wait()
    c_c.wait_recv()
    c_hc.wait_recv()
    keys = jnp.concatenate([cot[k, i, j] for i in range(NH) for j in range(NX) for k in range(NC)], axis=0)
    for i in range(4):
        rows = slice(i * 128, i * 128 + 128)
        grad = lax.dot_general(h[:, rows], keys, (((0,), (0,)), ((), ())), preferred_element_type=F32)
        first = beta_one * m[rows].astype(F32) + (1.0 - beta_one) * grad
        second = beta_two * v[rows].astype(F32) + (1.0 - beta_two) * grad * grad
        weight = w[rows].astype(F32)
        update = first / corr_one / (jnp.sqrt(second / corr_two) + adam_eps) + decay_rate * weight
        nw_ref[rows] = (weight - inner_rate * update).astype(BF16)
        nm_ref[rows] = first.astype(BF16)
        nv_ref[rows] = second.astype(BF16)

    for copy in loads[6:]:
        copy.wait()
    for copy in f_yg:
        copy.wait_recv()
    for j in range(NY):
        for i in range(NZ // 2):
            r = (j // 2) * 16 + (i // 2) * 8
            q = (j % 2) * 256 + (i % 2) * 128
            area = (slice(r, r + 8), slice(q, q + 128))
            total = jnp.concatenate([yg[j, 2 * i], yg[j, 2 * i + 1]], axis=0)
            delta = g[area] - total * (1.0 / (NY * NZ))
            fresh = outer_mu * o[area] + delta
            no_ref[area] = fresh
            ng_ref[area] = g[area] - outer_rate * (delta + outer_mu * fresh)

    for copy in started:
        copy.wait_send()


def store_kernel(*refs):
    sems = refs[10]
    copies = [pltpu.make_async_copy(refs[i], refs[5 + i], sems.at[i]) for i in range(5)]
    for copy in copies:
        copy.start()
    for copy in copies:
        copy.wait()


def per_device(hidden, cotangent, weight, first, second, local, glob, momentum):
    hidden, cotangent, weight, first, second, local = (a[0] for a in (hidden, cotangent, weight, first, second, local))
    args = (hidden, cotangent, weight, first, second, local, glob, momentum)
    (tok, d), (ktok, kv), (rows, _) = hidden.shape, cotangent.shape, glob.shape
    vm = pl.BlockSpec(memory_space=pltpu.VMEM)
    out = pl.pallas_call(
        kernel,
        out_shape=[
            jax.ShapeDtypeStruct((d, kv), BF16),
            jax.ShapeDtypeStruct((d, kv), BF16),
            jax.ShapeDtypeStruct((d, kv), BF16),
            jax.ShapeDtypeStruct((rows, kv), F32),
            jax.ShapeDtypeStruct((rows, kv), F32),
        ],
        in_specs=[pl.BlockSpec(memory_space=pltpu.HBM)] * 8,
        out_specs=[vm] * 5,
        scratch_shapes=[
            pltpu.VMEM((tok, d), BF16),
            pltpu.VMEM((d, kv), BF16),
            pltpu.VMEM((d, kv), BF16),
            pltpu.VMEM((d, kv), BF16),
            pltpu.VMEM((rows, kv), F32),
            pltpu.VMEM((rows, kv), F32),
            pltpu.VMEM((NC, NH, NX, ktok, kv), BF16),
            pltpu.VMEM((NY, 16, 256), BF16),
            pltpu.VMEM((NZ, 4, 128), F32),
            pltpu.VMEM((NZ, 4, 128), F32),
            pltpu.VMEM((NZ, 4, 128), F32),
            pltpu.VMEM((NY, NZ, 4, 128), F32),
            pltpu.SemaphoreType.DMA((8,)),
            pltpu.SemaphoreType.DMA((9,)),
            pltpu.SemaphoreType.DMA((9,)),
            pltpu.SemaphoreType.DMA((28,)),
            pltpu.SemaphoreType.DMA((28,)),
        ],
        compiler_params=pltpu.CompilerParams(
            collective_id=0, has_side_effects=True, vmem_limit_bytes=24 * 1024 * 1024
        ),
    )(*(pltpu.with_memory_space_constraint(a, pltpu.HBM) for a in args))
    out = pl.pallas_call(
        store_kernel,
        out_shape=[jax.ShapeDtypeStruct(a.shape, a.dtype) for a in out],
        in_specs=[vm] * 5,
        out_specs=[pl.BlockSpec(memory_space=pltpu.HBM)] * 5,
        scratch_shapes=[pltpu.SemaphoreType.DMA((5,))],
    )(*out)
    return (out[0][None], out[1][None], out[2][None], out[3], out[4])


def solution(mesh):
    return jax.shard_map(
        per_device,
        mesh=mesh,
        in_specs=(
            P("replica", None, "tensor"),
            P("replica", "tensor", None),
            P("replica", "tensor", None),
            P("replica", "tensor", None),
            P("replica", "tensor", None),
            P("replica", "tensor", None),
            P("tensor", None),
            P("tensor", None),
        ),
        out_specs=(
            P("replica", "tensor", None),
            P("replica", "tensor", None),
            P("replica", "tensor", None),
            P("tensor", None),
            P("tensor", None),
        ),
        check_vma=False,
    )
```

time: 833 us -> 50.1 us (0.06)
  the two profiles are of different devices: /device:TPU:4 before, /device:TPU:22 now
where the time goes in v1:
time: 50.1 us; the launch traced here: 49.9 us
  Pallas kernels  45.6 us (91%)
  local copies, waits for them, and re-layouts  3.68 us (7%)
  between operations  0.65 us (1%)
    pallas_call x1, Pallas kernels, per_device(): pl.pallas_call(kernel, out_shape=[jax.ShapeDtypeStruct((d, kv), BF16), ja...  42.9 us
    unnamed x10, local copies, waits for them, and re-layouts  3.68 us
    pallas_call x1, Pallas kernels, per_device(): pl.pallas_call(store_kernel, out_shape=[jax.ShapeDtypeStruct(a.shape, a.d...  2.67 us

profile of v1, /device:TPU:22, one launch (start us, length us, event | category | flops | bytes accessed | tf_op | source)
XLA Modules:
  0.0 49.9 jit_solution(14869029053351863402)
XLA Ops:
  0.6 42.9 %shard_map.119 = (bf16[512,512]{1,0:T(8,128)(2,1)S(1)}, bf16[512,512]{1,0:T(8,128)(2,1)S(1)}, bf16[512,512]{1,0:T(8,128)(2,1)S(1)}, f32[64,512]{1,0:T(8,128)S(1)}, f32[64,512]{1,0:T(8,128)S(1)}) custom-call(bf16[256,512]{1,0:T(8,128)(2,1)} %bitcast.12, bf16[16,512]{1,0:T(8,128)(2,1)} %bitcast.14, bf16[512,512]{1,0:T(8,128)(2,1)} %bitcast.9, ...), custom_call_target="tpu_custom_call" | custom-call | tf_op jit(solution)/shard_map/pallas_call | solution.py:181
  43.6 0.0 copy-start
  43.6 0.8 %copy-done = bf16[512,512]{1,0:T(8,128)(2,1)} copy-done((bf16[512,512]{1,0:T(8,128)(2,1)}, bf16[512,512]{1,0:T(8,128)(2,1)S(1)}, u32[]{:S(2)}) %copy-start) | copy-done | bytes 524312
  44.4 0.0 copy-start.1
  44.4 0.8 %copy-done.1 = bf16[512,512]{1,0:T(8,128)(2,1)} copy-done((bf16[512,512]{1,0:T(8,128)(2,1)}, bf16[512,512]{1,0:T(8,128)(2,1)S(1)}, u32[]{:S(2)}) %copy-start.1) | copy-done | bytes 524312
  45.1 0.0 copy-start.2
  45.1 0.8 %copy-done.2 = bf16[512,512]{1,0:T(8,128)(2,1)} copy-done((bf16[512,512]{1,0:T(8,128)(2,1)}, bf16[512,512]{1,0:T(8,128)(2,1)S(1)}, u32[]{:S(2)}) %copy-start.2) | copy-done | bytes 524312
  45.9 0.0 copy-start.3
  45.9 0.7 %copy-done.3 = f32[64,512]{1,0:T(8,128)} copy-done((f32[64,512]{1,0:T(8,128)}, f32[64,512]{1,0:T(8,128)S(1)}, u32[]{:S(2)}) %copy-start.3) | copy-done | bytes 131096
  46.6 0.0 copy-start.4
  46.6 0.6 %copy-done.4 = f32[64,512]{1,0:T(8,128)} copy-done((f32[64,512]{1,0:T(8,128)}, f32[64,512]{1,0:T(8,128)S(1)}, u32[]{:S(2)}) %copy-start.4) | copy-done | bytes 131096
  47.2 2.7 %shard_map.120 = (bf16[512,512]{1,0:T(8,128)(2,1)}, bf16[512,512]{1,0:T(8,128)(2,1)}, bf16[512,512]{1,0:T(8,128)(2,1)}, f32[64,512]{1,0:T(8,128)}, f32[64,512]{1,0:T(8,128)}) custom-call(bf16[512,512]{1,0:T(8,128)(2,1)} %copy-done, bf16[512,512]{1,0:T(8,128)(2,1)} %copy-done.1, bf16[512,512]{1,0:T(8,128)(2,1)} %copy-done.2, f32[64,512]{1,0:T(8,128)} %copy-done.3, ...), custom_call_target="tpu_custom_call" | custom-call | tf_op jit(solution)/shard_map/pallas_call | solution.py:215
Async XLA Ops:
  43.6 0.8 %copy-start = (bf16[512,512]{1,0:T(8,128)(2,1)}, bf16[512,512]{1,0:T(8,128)(2,1)S(1)}, u32[]{:S(2)}) copy-start(bf16[512,512]{1,0:T(8,128)(2,1)S(1)} %get-tuple-element.15.refs_0_) | copy-start | bytes 1572868
  44.4 0.8 %copy-start.1 = (bf16[512,512]{1,0:T(8,128)(2,1)}, bf16[512,512]{1,0:T(8,128)(2,1)S(1)}, u32[]{:S(2)}) copy-start(bf16[512,512]{1,0:T(8,128)(2,1)S(1)} %get-tuple-element.16.refs_1_) | copy-start | bytes 1572868
  45.1 0.8 %copy-start.2 = (bf16[512,512]{1,0:T(8,128)(2,1)}, bf16[512,512]{1,0:T(8,128)(2,1)S(1)}, u32[]{:S(2)}) copy-start(bf16[512,512]{1,0:T(8,128)(2,1)S(1)} %get-tuple-element.17.refs_2_) | copy-start | bytes 1572868
  45.9 0.7 %copy-start.3 = (f32[64,512]{1,0:T(8,128)}, f32[64,512]{1,0:T(8,128)S(1)}, u32[]{:S(2)}) copy-start(f32[64,512]{1,0:T(8,128)S(1)} %get-tuple-element.18.refs_3_) | copy-start | bytes 393220
  46.6 0.6 %copy-start.4 = (f32[64,512]{1,0:T(8,128)}, f32[64,512]{1,0:T(8,128)S(1)}, u32[]{:S(2)}) copy-start(f32[64,512]{1,0:T(8,128)S(1)} %get-tuple-element.19.refs_4_) | copy-start | bytes 393220

commit v2 on v1

--- a/solution.py
+++ b/solution.py
@@ -25,18 +25,26 @@
 def kernel(
     h_hbm, k_hbm, w_hbm, m_hbm, v_hbm, l_hbm, g_hbm, o_hbm,
     nw_ref, nm_ref, nv_ref, ng_ref, no_ref,
-    h, w, m, v, g, o, cot, yb, part, zb, zg, yg,
-    load_sem, send_c, recv_c, send_f, recv_f,
+    h, w, m, v, g, o, cot, raw, part, sums, whole,
+    load_sem, send_c, recv_c, send_r, recv_r, send_s, recv_s, send_w, recv_w,
 ):
     rep, ten = lax.axis_index("replica"), lax.axis_index("tensor")
     zl, y = rep // NY, lax.rem(rep, NY)
     zh, x, c = ten // (NX * NC), lax.rem(ten // NC, NX), lax.rem(ten, NC)
-
-    def at_y(k):
-        return (zl * NY + lax.rem(y + k, NY), ten)
-
-    def at_z(k):
-        return (lax.rem(zl + k, NZ) * NY + y, ten)
+    pair, side = zl // 2, lax.rem(zl, 2)
+    me = y * 2 + side
+
+    near = sorted(((k, e) for k in range(NY) for e in range(2) if k + e > 0), key=lambda t: -(min(t[0], NY - t[0]) + t[1]))
+
+    def place(k, e):
+        return lax.rem(y + k, NY), (1 - side if e else side)
+
+    def at_near(k, e):
+        yy, ss = place(k, e)
+        return ((pair * 2 + ss) * NY + yy, ten)
+
+    def at_pair(k):
+        return ((lax.rem(pair + k, NZ // 2) * 2 + side) * NY + y, ten)
 
     def at_x(k):
         return (rep, zh * NX * NC + lax.rem(x + k, NX) * NC + c)
@@ -45,19 +53,20 @@
     at_c = (rep, zh * NX * NC + x * NC + 1 - c)
 
     barrier = pltpu.get_barrier_semaphore()
-    partners = [at_y(k) for k in range(1, NY)] + [at_z(k) for k in range(1, NZ)] + [at_x(k) for k in range(1, NX)] + [at_h, at_c]
+    partners = [at_h] + [at_pair(k) for k in range(1, NZ // 2)] + [at_near(*t) for t in near] + [at_x(k) for k in (2, 1, 3)] + [at_c]
     for partner in partners:
         pl.semaphore_signal(barrier, inc=1, device_id=partner, device_id_type=MESH)
 
-    def chunk(k):
-        yy = lax.rem(y + k, NY)
-        return l_hbm.at[pl.ds(pl.multiple_of((yy // 2) * 16, 16), 16), pl.ds(pl.multiple_of(lax.rem(yy, 2) * 256, 256), 256)]
+    def chunk(k, e):
+        yy, ss = place(k, e)
+        i = yy * 2 + ss
+        return l_hbm.at[pl.ds(pl.multiple_of((i // 4) * 16, 16), 16), pl.ds(pl.multiple_of(lax.rem(i, 4) * 128, 128), 128)]
 
     loads = [
         pltpu.make_async_copy(src, dst, load_sem.at[i])
         for i, (src, dst) in enumerate(
             [
-                (chunk(0), yb.at[y]),
+                (chunk(0, 0), raw.at[me]),
                 (k_hbm, cot.at[c, zh, x]),
                 (h_hbm, h),
                 (w_hbm, w),
@@ -74,60 +83,51 @@
 
     started = []
 
-    def send(src, dst, sems, i, device):
+    def send(src, dst, sends, recvs, i, device):
         copy = pltpu.make_async_remote_copy(
-            src_ref=src, dst_ref=dst, send_sem=sems[0].at[i], recv_sem=sems[1].at[i], device_id=device, device_id_type=MESH
+            src_ref=src, dst_ref=dst, send_sem=sends.at[i], recv_sem=recvs.at[i], device_id=device, device_id_type=MESH
         )
         copy.start()
         started.append(copy)
         return copy
 
-    sc, sf = (send_c, recv_c), (send_f, recv_f)
     mine = cot.at[c, zh, x]
     theirs = cot.at[c, 1 - zh, x]
-    c_h = send(k_hbm, mine, sc, 0, at_h)
-    f_y = [send(chunk(k), yb.at[y], sf, k - 1, at_y(k)) for k in range(1, NY)]
-    c_x = [send(k_hbm, mine, sc, k, at_x(k)) for k in range(1, NX)]
+    c_h = send(k_hbm, mine, send_c, recv_c, 0, at_h)
+    f_raw = [send(chunk(*t), raw.at[me], send_r, recv_r, t[0] * 2 + t[1] - 1, at_near(*t)) for t in near]
+    c_x = [send(k_hbm, mine, send_c, recv_c, k, at_x(k)) for k in (2, 1, 3)]
 
     loads[0].wait()
-    for copy in f_y:
-        copy.wait_recv()
-    total = yb[0].astype(F32)
-    for i in range(1, NY):
-        total += yb[i].astype(F32)
-    for i in range(NZ):
-        r, q, s = i // 4, (i // 2) % 2, i % 2
-        part[i] = total[r * 8 + s * 4 : r * 8 + s * 4 + 4, q * 128 : q * 128 + 128]
-    f_z = [send(part.at[lax.rem(zl + k, NZ)], zb.at[zl], sf, 7 + k - 1, at_z(k)) for k in range(1, NZ)]
+    for copy in f_raw:
+        copy.wait_recv()
+    total = raw[0].astype(F32)
+    for i in range(1, 2 * NY):
+        total += raw[i].astype(F32)
+    part[...] = total
+    f_sum = [send(part, sums.at[pair], send_s, recv_s, k - 1, at_pair(k)) for k in range(1, NZ // 2)]
+    sums[pair] = total
 
     c_h.wait_recv()
-    c_hx = [send(theirs, theirs, sc, 3 + k, at_x(k)) for k in range(1, NX)]
+    c_hx = [send(theirs, theirs, send_c, recv_c, 3 + k, at_x(k)) for k in (2, 1, 3)]
 
     loads[1].wait()
     for copy in c_x:
         copy.wait_recv()
     row = cot.at[c, zh]
-    c_c = send(row, row, sc, 7, at_c)
-
-    for copy in f_z:
-        copy.wait_recv()
-    zb[zl] = part[zl]
-    total = zb[0]
-    for i in range(1, NZ):
-        total += zb[i]
-    zg[zl] = total
-    f_zg = [send(zg.at[zl], zg.at[zl], sf, 14 + k - 1, at_z(k)) for k in range(1, NZ)]
+    c_c = send(row, row, send_c, recv_c, 7, at_c)
+
+    for copy in f_sum:
+        copy.wait_recv()
+    total = sums[0]
+    for i in range(1, NZ // 2):
+        total += sums[i]
+    whole[me] = total
+    f_whole = [send(whole.at[me], whole.at[me], send_w, recv_w, t[0] * 2 + t[1] - 1, at_near(*t)) for t in near]
 
     for copy in c_hx:
         copy.wait_recv()
     row = cot.at[c, 1 - zh]
-    c_hc = send(row, row, sc, 8, at_c)
-
-    for copy in f_zg:
-        copy.wait_recv()
-    f_yg = [send(zg, yg.at[y], sf, 21 + k - 1, at_y(k)) for k in range(1, NY)]
-    for i in range(NZ):
-        yg[y, i] = zg[i]
+    c_hc = send(row, row, send_c, recv_c, 8, at_c)
 
     for copy in loads[2:6]:
         copy.wait()
@@ -147,18 +147,15 @@
 
     for copy in loads[6:]:
         copy.wait()
-    for copy in f_yg:
-        copy.wait_recv()
-    for j in range(NY):
-        for i in range(NZ // 2):
-            r = (j // 2) * 16 + (i // 2) * 8
-            q = (j % 2) * 256 + (i % 2) * 128
-            area = (slice(r, r + 8), slice(q, q + 128))
-            total = jnp.concatenate([yg[j, 2 * i], yg[j, 2 * i + 1]], axis=0)
-            delta = g[area] - total * (1.0 / (NY * NZ))
-            fresh = outer_mu * o[area] + delta
-            no_ref[area] = fresh
-            ng_ref[area] = g[area] - outer_rate * (delta + outer_mu * fresh)
+    for copy in f_whole:
+        copy.wait_recv()
+    for i in range(2 * NY):
+        r, q = (i // 4) * 16, (i % 4) * 128
+        area = (slice(r, r + 16), slice(q, q + 128))
+        delta = g[area] - whole[i] * (1.0 / (NY * NZ))
+        fresh = outer_mu * o[area] + delta
+        no_ref[area] = fresh
+        ng_ref[area] = g[area] - outer_rate * (delta + outer_mu * fresh)
 
     for copy in started:
         copy.wait_send()
@@ -197,19 +194,22 @@
             pltpu.VMEM((rows, kv), F32),
             pltpu.VMEM((rows, kv), F32),
             pltpu.VMEM((NC, NH, NX, ktok, kv), BF16),
-            pltpu.VMEM((NY, 16, 256), BF16),
-            pltpu.VMEM((NZ, 4, 128), F32),
-            pltpu.VMEM((NZ, 4, 128), F32),
-            pltpu.VMEM((NZ, 4, 128), F32),
-            pltpu.VMEM((NY, NZ, 4, 128), F32),
+            pltpu.VMEM((2 * NY, 16, 128), BF16),
+            pltpu.VMEM((16, 128), F32),
+            pltpu.VMEM((NZ // 2, 16, 128), F32),
+            pltpu.VMEM((2 * NY, 16, 128), F32),
             pltpu.SemaphoreType.DMA((8,)),
             pltpu.SemaphoreType.DMA((9,)),
             pltpu.SemaphoreType.DMA((9,)),
-            pltpu.SemaphoreType.DMA((28,)),
-            pltpu.SemaphoreType.DMA((28,)),
+            pltpu.SemaphoreType.DMA((15,)),
+            pltpu.SemaphoreType.DMA((15,)),
+            pltpu.SemaphoreType.DMA((3,)),
+            pltpu.SemaphoreType.DMA((3,)),
+            pltpu.SemaphoreType.DMA((15,)),
+            pltpu.SemaphoreType.DMA((15,)),
         ],
         compiler_params=pltpu.CompilerParams(
-            collective_id=0, has_side_effects=True, vmem_limit_bytes=24 * 1024 * 1024
+            collective_id=0, has_side_effects=True, vmem_limit_bytes=16 * 1024 * 1024
         ),
     )(*(pltpu.with_memory_space_constraint(a, pltpu.HBM) for a in args))
     out = pl.pallas_call(
@@ -218,6 +218,7 @@
         in_specs=[vm] * 5,
         out_specs=[pl.BlockSpec(memory_space=pltpu.HBM)] * 5,
         scratch_shapes=[pltpu.SemaphoreType.DMA((5,))],
+        compiler_params=pltpu.CompilerParams(vmem_limit_bytes=4 * 1024 * 1024),
     )(*out)
     return (out[0][None], out[1][None], out[2][None], out[3], out[4])
 

time: 50.1 us -> 42 us (0.84)
  the two profiles are of different devices: /device:TPU:22 before, /device:TPU:1 now
where the time goes in v2:
time: 42 us; the launch traced here: 41.5 us
  Pallas kernels  40.8 us (97%)
  between operations  0.64 us (2%)
    pallas_call x1, Pallas kernels, per_device(): pl.pallas_call(kernel, out_shape=[jax.ShapeDtypeStruct((d, kv), BF16), ja...  39.6 us
    pallas_call x1, Pallas kernels, per_device(): pl.pallas_call(store_kernel, out_shape=[jax.ShapeDtypeStruct(a.shape, a.d...  1.26 us

profile of v2, /device:TPU:1, one launch (start us, length us, event | category | flops | bytes accessed | tf_op | source)
XLA Modules:
  0.0 41.5 jit_solution(8501532093626519348)
XLA Ops:
  0.6 39.6 %shard_map.119 = (bf16[512,512]{1,0:T(8,128)(2,1)S(1)}, bf16[512,512]{1,0:T(8,128)(2,1)S(1)}, bf16[512,512]{1,0:T(8,128)(2,1)S(1)}, f32[64,512]{1,0:T(8,128)S(1)}, f32[64,512]{1,0:T(8,128)S(1)}) custom-call(bf16[256,512]{1,0:T(8,128)(2,1)} %bitcast.12, bf16[16,512]{1,0:T(8,128)(2,1)} %bitcast.14, bf16[512,512]{1,0:T(8,128)(2,1)} %bitcast.9, ...), custom_call_target="tpu_custom_call" | custom-call | tf_op jit(solution)/shard_map/pallas_call | solution.py:178
  40.2 1.3 %shard_map.120 = (bf16[512,512]{1,0:T(8,128)(2,1)}, bf16[512,512]{1,0:T(8,128)(2,1)}, bf16[512,512]{1,0:T(8,128)(2,1)}, f32[64,512]{1,0:T(8,128)}, f32[64,512]{1,0:T(8,128)}) custom-call(bf16[512,512]{1,0:T(8,128)(2,1)S(1)} %get-tuple-element.15.refs_0_, bf16[512,512]{1,0:T(8,128)(2,1)S(1)} %get-tuple-element.16.refs_1_, ...), custom_call_target="tpu_custom_call" | custom-call | tf_op jit(solution)/shard_map/pallas_call | solution.py:215

commit v3 on v2

v3 whole, which is shorter than its diff:
```python
import jax
import jax.numpy as jnp
from jax import lax
from jax.experimental import pallas as pl
from jax.experimental.pallas import tpu as pltpu
from jax.sharding import PartitionSpec as P

ADAM_STEP = 4
beta_one = 0.9
beta_two = 0.95
adam_eps = 1e-08
inner_rate = 0.01
decay_rate = 0.1
outer_rate = 0.7
outer_mu = 0.9
corr_one = 1.0 - beta_one**ADAM_STEP
corr_two = 1.0 - beta_two**ADAM_STEP

MESH = pl.DeviceIdType.MESH
NY, NZ, NX, NH, NC = 8, 8, 4, 2, 2
NR = 2
F32 = jnp.float32
BF16 = jnp.bfloat16


def kernel(
    h_hbm, k_hbm, w_hbm, m_hbm, v_hbm, l_hbm, g_hbm, o_hbm,
    nw_ref, nm_ref, nv_ref, ng_ref, no_ref,
    h, w, m, v, g, o, cot, raw, whole,
    load_sem, send_c, recv_c, send_r, recv_r, send_w, recv_w, send_z, recv_z, send_y, recv_y, ready,
):
    rep, ten = lax.axis_index("replica"), lax.axis_index("tensor")
    zl, y = rep // NY, lax.rem(rep, NY)
    zh, x, c = ten // (NX * NC), lax.rem(ten // NC, NX), lax.rem(ten, NC)
    side = lax.rem(zl, NR)
    reducer = zl < NR
    me = y * NR + side

    near = sorted(((k, e) for k in range(NY) for e in range(NR) if k + e > 0), key=lambda t: -(min(t[0], NY - t[0]) + t[1]))

    def place(k, e):
        return lax.rem(y + k, NY), (1 - side if e else side)

    def at_near(k, e):
        yy, ss = place(k, e)
        return (ss * NY + yy, ten)

    def at_y(k):
        return (zl * NY + lax.rem(y + k, NY), ten)

    def at_x(k, other=False):
        return (rep, zh * NX * NC + lax.rem(x + k, NX) * NC + (1 - c if other else c))

    at_h = (rep, (1 - zh) * NX * NC + x * NC + c)

    barrier = pltpu.get_barrier_semaphore()

    @pl.when(zh == 0)
    def _():
        pl.semaphore_signal(barrier, inc=1, device_id=at_h, device_id_type=MESH)

    peers = [at_x(k, other) for k in (2, 1, 3, 0) for other in (False, True) if k or other]
    for peer in peers:
        pl.semaphore_signal(barrier, inc=1, device_id=peer, device_id_type=MESH)

    @pl.when(reducer)
    def _():
        for t in near:
            pl.semaphore_signal(barrier, inc=1, device_id=at_near(*t), device_id_type=MESH)
        for z in range(NR, NZ):
            for i in range(NY):
                pl.semaphore_signal(barrier, inc=1, device_id=(z * NY + i, ten), device_id_type=MESH)

    def chunk(k, e):
        yy, ss = place(k, e)
        i = yy * NR + ss
        return l_hbm.at[pl.ds(pl.multiple_of((i // 4) * 16, 16), 16), pl.ds(pl.multiple_of(lax.rem(i, 4) * 128, 128), 128)]

    loads = [
        pltpu.make_async_copy(src, dst, load_sem.at[i])
        for i, (src, dst) in enumerate([(k_hbm, cot.at[c, zh, x]), (h_hbm, h), (w_hbm, w), (m_hbm, m), (v_hbm, v), (g_hbm, g), (o_hbm, o)])
    ]
    for copy in loads:
        copy.start()

    own = pltpu.make_async_copy(chunk(0, 0), raw.at[rep], load_sem.at[7])

    @pl.when(reducer)
    def _():
        own.start()

    pl.semaphore_wait(barrier, NY * NR - reducer.astype(jnp.int32) + len(peers) + zh)

    def make(src, dst, sends, recvs, i, j, device):
        return pltpu.make_async_remote_copy(
            src_ref=src, dst_ref=dst, send_sem=sends.at[i], recv_sem=recvs.at[j], device_id=device, device_id_type=MESH
        )

    mine = cot.at[c, zh, x]
    theirs = cot.at[c, 1 - zh, x]
    c_h = make(k_hbm, mine, send_c, recv_c, 0, 0, at_h)
    c_x = [make(k_hbm, mine, send_c, recv_c, k, k, at_x(k)) for k in (2, 1, 3)]
    both = [(k, other) for k in (2, 1, 3, 0) for other in (False, True) if k or other]
    c_hx = [make(theirs, theirs, send_c, recv_c, 4 + i, 4 + i, at_x(*t)) for i, t in enumerate(both)]
    row = cot.at[c, zh]
    c_c = make(row, row, send_c, recv_c, 11, 11, at_x(0, True))

    @pl.when(zh == 1)
    def _():
        c_h.start()
        pl.semaphore_signal(ready, inc=1, device_id=at_h, device_id_type=MESH)

    f_raw = [make(chunk(*t), raw.at[rep], send_r, recv_r, t[0] * NR + t[1], rep, at_near(*t)) for t in near]
    f_own = make(chunk(0, 0), raw.at[rep], send_r, recv_r, 0, rep, at_near(0, 0))
    for copy in f_raw:
        copy.start()

    @pl.when(jnp.logical_not(reducer))
    def _():
        f_own.start()

    for copy in c_x:
        copy.start()
    loads[0].wait()
    for copy in c_x:
        copy.wait_recv()
    c_c.start()

    f_whole = [make(whole.at[me], whole.at[me], send_w, recv_w, t[0] * NR + t[1], t[0] * NR + t[1], at_near(*t)) for t in near]
    f_z = [make(whole.at[me], whole.at[me], send_z, recv_z, z, side, (z * NY + y, ten)) for z in range(NR, NZ)]

    @pl.when(reducer)
    def _():
        own.wait()

        def plane(z, total):
            for i in range(NY):
                slot = z * NY + i

                @pl.when(slot != rep)
                def _():
                    make(raw.at[slot], raw.at[slot], send_r, recv_r, 0, slot, at_near(0, 1)).wait_recv()

            for i in range(NY):
                total += raw[z * NY + i].astype(F32)
            return total

        whole[me] = lax.fori_loop(0, NZ, plane, jnp.zeros((16, 128), F32))
        for copy in f_whole:
            copy.start()
        for copy in f_z:
            copy.start()

    @pl.when(zh == 0)
    def _():
        pl.semaphore_wait(ready, 1)
        c_h.start()

    c_h.wait_recv()
    for copy in c_hx:
        copy.start()

    both_chunks = whole.at[pl.ds(y * NR, NR)]
    f_y = [make(both_chunks, both_chunks, send_y, recv_y, k, k, at_y(k)) for k in (4, 3, 5, 2, 6, 1, 7)]

    @pl.when(jnp.logical_not(reducer))
    def _():
        for i in range(NR):
            slot = whole.at[y * NR + i]
            make(slot, slot, send_z, recv_z, 0, i, at_near(0, 0)).wait_recv()
        for copy in f_y:
            copy.start()

    for copy in loads[1:5]:
        copy.wait()
    c_c.wait_recv()
    for copy in c_hx:
        copy.wait_recv()
    keys = jnp.concatenate([cot[k, i, j] for i in range(NH) for j in range(NX) for k in range(NC)], axis=0)
    for i in range(4):
        rows = slice(i * 128, i * 128 + 128)
        grad = lax.dot_general(h[:, rows], keys, (((0,), (0,)), ((), ())), preferred_element_type=F32)
        first = beta_one * m[rows].astype(F32) + (1.0 - beta_one) * grad
        second = beta_two * v[rows].astype(F32) + (1.0 - beta_two) * grad * grad
        weight = w[rows].astype(F32)
        update = first / corr_one / (jnp.sqrt(second / corr_two) + adam_eps) + decay_rate * weight
        nw_ref[rows] = (weight - inner_rate * update).astype(BF16)
        nm_ref[rows] = first.astype(BF16)
        nv_ref[rows] = second.astype(BF16)

    for copy in loads[5:]:
        copy.wait()

    @pl.when(reducer)
    def _():
        for copy in f_whole:
            copy.wait_recv()

    @pl.when(jnp.logical_not(reducer))
    def _():
        for copy in f_y:
            copy.wait_recv()

    for i in range(NR * NY):
        r, q = (i // 4) * 16, (i % 4) * 128
        area = (slice(r, r + 16), slice(q, q + 128))
        delta = g[area] - whole[i] * (1.0 / (NY * NZ))
        fresh = outer_mu * o[area] + delta
        no_ref[area] = fresh
        ng_ref[area] = g[area] - outer_rate * (delta + outer_mu * fresh)

    for copy in [c_h, c_c] + c_x + c_hx + f_raw:
        copy.wait_send()

    @pl.when(reducer)
    def _():
        for copy in f_whole + f_z:
            copy.wait_send()

    @pl.when(jnp.logical_not(reducer))
    def _():
        for copy in [f_own] + f_y:
            copy.wait_send()


def store_kernel(*refs):
    sems = refs[10]
    copies = [pltpu.make_async_copy(refs[i], refs[5 + i], sems.at[i]) for i in range(5)]
    for copy in copies:
        copy.start()
    for copy in copies:
        copy.wait()


def per_device(hidden, cotangent, weight, first, second, local, glob, momentum):
    hidden, cotangent, weight, first, second, local = (a[0] for a in (hidden, cotangent, weight, first, second, local))
    args = (hidden, cotangent, weight, first, second, local, glob, momentum)
    (tok, d), (ktok, kv), (rows, _) = hidden.shape, cotangent.shape, glob.shape
    vm = pl.BlockSpec(memory_space=pltpu.VMEM)
    out = pl.pallas_call(
        kernel,
        out_shape=[
            jax.ShapeDtypeStruct((d, kv), BF16),
            jax.ShapeDtypeStruct((d, kv), BF16),
            jax.ShapeDtypeStruct((d, kv), BF16),
            jax.ShapeDtypeStruct((rows, kv), F32),
            jax.ShapeDtypeStruct((rows, kv), F32),
        ],
        in_specs=[pl.BlockSpec(memory_space=pltpu.HBM)] * 8,
        out_specs=[vm] * 5,
        scratch_shapes=[
            pltpu.VMEM((tok, d), BF16),
            pltpu.VMEM((d, kv), BF16),
            pltpu.VMEM((d, kv), BF16),
            pltpu.VMEM((d, kv), BF16),
            pltpu.VMEM((rows, kv), F32),
            pltpu.VMEM((rows, kv), F32),
            pltpu.VMEM((NC, NH, NX, ktok, kv), BF16),
            pltpu.VMEM((NY * NZ, 16, 128), BF16),
            pltpu.VMEM((NR * NY, 16, 128), F32),
            pltpu.SemaphoreType.DMA((8,)),
            pltpu.SemaphoreType.DMA((12,)),
            pltpu.SemaphoreType.DMA((12,)),
            pltpu.SemaphoreType.DMA((16,)),
            pltpu.SemaphoreType.DMA((NY * NZ,)),
            pltpu.SemaphoreType.DMA((16,)),
            pltpu.SemaphoreType.DMA((16,)),
            pltpu.SemaphoreType.DMA((NZ,)),
            pltpu.SemaphoreType.DMA((NR,)),
            pltpu.SemaphoreType.DMA((NY,)),
            pltpu.SemaphoreType.DMA((NY,)),
            pltpu.SemaphoreType.REGULAR,
        ],
        compiler_params=pltpu.CompilerParams(
            collective_id=0, has_side_effects=True, vmem_limit_bytes=16 * 1024 * 1024
        ),
    )(*(pltpu.with_memory_space_constraint(a, pltpu.HBM) for a in args))
    out = pl.pallas_call(
        store_kernel,
        out_shape=[jax.ShapeDtypeStruct(a.shape, a.dtype) for a in out],
        in_specs=[vm] * 5,
        out_specs=[pl.BlockSpec(memory_space=pltpu.HBM)] * 5,
        scratch_shapes=[pltpu.SemaphoreType.DMA((5,))],
        compiler_params=pltpu.CompilerParams(vmem_limit_bytes=4 * 1024 * 1024),
    )(*out)
    return (out[0][None], out[1][None], out[2][None], out[3], out[4])


def solution(mesh):
    return jax.shard_map(
        per_device,
        mesh=mesh,
        in_specs=(
            P("replica", None, "tensor"),
            P("replica", "tensor", None),
            P("replica", "tensor", None),
            P("replica", "tensor", None),
            P("replica", "tensor", None),
            P("replica", "tensor", None),
            P("tensor", None),
            P("tensor", None),
        ),
        out_specs=(
            P("replica", "tensor", None),
            P("replica", "tensor", None),
            P("replica", "tensor", None),
            P("tensor", None),
            P("tensor", None),
        ),
        check_vma=False,
    )
```

time: 42 us -> 37.9 us (0.902)
  Pallas kernels: 40.8 us -> 37.1 us
    pallas_call x1, Pallas kernels: 39.6 us -> 35.8 us  [per_device(): pl.pallas_call(kernel, out_shape=[jax.ShapeDtypeStruct((d, kv), BF16), ja...]
where the time goes in v3:
time: 37.9 us; the launch traced here: 37.7 us
  Pallas kernels  37.1 us (98%)
  between operations  0.64 us (2%)
    pallas_call x1, Pallas kernels, per_device(): pl.pallas_call(kernel, out_shape=[jax.ShapeDtypeStruct((d, kv), BF16), ja...  35.8 us
    pallas_call x1, Pallas kernels, per_device(): pl.pallas_call(store_kernel, out_shape=[jax.ShapeDtypeStruct(a.shape, a.d...  1.26 us

profile of v3, /device:TPU:1, one launch (start us, length us, event | category | flops | bytes accessed | tf_op | source)
XLA Modules:
  0.0 37.7 jit_solution(5546230481322938274)
XLA Ops:
  0.6 35.8 %shard_map.119 = (bf16[512,512]{1,0:T(8,128)(2,1)S(1)}, bf16[512,512]{1,0:T(8,128)(2,1)S(1)}, bf16[512,512]{1,0:T(8,128)(2,1)S(1)}, f32[64,512]{1,0:T(8,128)S(1)}, f32[64,512]{1,0:T(8,128)S(1)}) custom-call(bf16[256,512]{1,0:T(8,128)(2,1)} %bitcast.12, bf16[16,512]{1,0:T(8,128)(2,1)} %bitcast.14, bf16[512,512]{1,0:T(8,128)(2,1)} %bitcast.9, ...), custom_call_target="tpu_custom_call" | custom-call | tf_op jit(solution)/shard_map/pallas_call | solution.py:240
  36.4 1.3 %shard_map.120 = (bf16[512,512]{1,0:T(8,128)(2,1)}, bf16[512,512]{1,0:T(8,128)(2,1)}, bf16[512,512]{1,0:T(8,128)(2,1)}, f32[64,512]{1,0:T(8,128)}, f32[64,512]{1,0:T(8,128)}) custom-call(bf16[512,512]{1,0:T(8,128)(2,1)S(1)} %get-tuple-element.15.refs_0_, bf16[512,512]{1,0:T(8,128)(2,1)S(1)} %get-tuple-element.16.refs_1_, ...), custom_call_target="tpu_custom_call" | custom-call | tf_op jit(solution)/shard_map/pallas_call | solution.py:278

commit v4 on v3

--- a/solution.py
+++ b/solution.py
@@ -19,6 +19,7 @@
 MESH = pl.DeviceIdType.MESH
 NY, NZ, NX, NH, NC = 8, 8, 4, 2, 2
 NR = 2
+HUB = 4
 F32 = jnp.float32
 BF16 = jnp.bfloat16
 
@@ -26,15 +27,29 @@
 def kernel(
     h_hbm, k_hbm, w_hbm, m_hbm, v_hbm, l_hbm, g_hbm, o_hbm,
     nw_ref, nm_ref, nv_ref, ng_ref, no_ref,
-    h, w, m, v, g, o, cot, raw, whole,
-    load_sem, send_c, recv_c, send_r, recv_r, send_w, recv_w, send_z, recv_z, send_y, recv_y, ready,
+    h, w, m, v, g, o, cot, raw, part, sums, whole,
+    load_sem, send_c, recv_c, send_r, recv_r, send_w, recv_w, send_z, recv_z, send_y, recv_y, send_s, recv_s, send_d, recv_d, ready, go,
 ):
     rep, ten = lax.axis_index("replica"), lax.axis_index("tensor")
     zl, y = rep // NY, lax.rem(rep, NY)
     zh, x, c = ten // (NX * NC), lax.rem(ten // NC, NX), lax.rem(ten, NC)
-    side = lax.rem(zl, NR)
-    reducer = zl < NR
+    upper = zh == 1
+    lower = zh == 0
+    pair = zl // 2
+    low = jnp.where(upper, pair * 2, jnp.where(ten == 0, 1, 0))
+    side = zl - low
+    inside = jnp.logical_and(side >= 0, side < NR)
+    reducer = jnp.logical_and(lower, inside)
+    plain = jnp.logical_and(lower, jnp.logical_not(inside))
+    direct = jnp.logical_and(lower, side < 0)
+    column = jnp.logical_and(lower, side >= NR)
+    side = lax.rem(zl + jnp.where(upper, 0, low), NR)
     me = y * NR + side
+    quick = jnp.logical_and(upper, zl < HUB)
+    hub = jnp.logical_and(upper, pair == HUB // 2)
+    last = jnp.logical_and(upper, pair == HUB // 2 + 1)
+    greets = jnp.logical_or(upper, zl < NR + 1)
+    first_plain = 3
 
     near = sorted(((k, e) for k in range(NY) for e in range(NR) if k + e > 0), key=lambda t: -(min(t[0], NY - t[0]) + t[1]))
 
@@ -43,33 +58,70 @@
 
     def at_near(k, e):
         yy, ss = place(k, e)
-        return (ss * NY + yy, ten)
+        return ((low + ss) * NY + yy, ten)
 
     def at_y(k):
         return (zl * NY + lax.rem(y + k, NY), ten)
 
-    def at_x(k, other=False):
-        return (rep, zh * NX * NC + lax.rem(x + k, NX) * NC + (1 - c if other else c))
+    def at_x(k, other=False, half=zh):
+        return (rep, half * NX * NC + lax.rem(x + k, NX) * NC + (1 - c if other else c))
+
+    def at_pair(k):
+        return ((lax.rem(pair + k, NZ // 2) * 2 + side) * NY + y, ten)
+
+    def at_z(z):
+        return (jnp.where(z < low, z, z + NR) * NY + y, ten)
 
     at_h = (rep, (1 - zh) * NX * NC + x * NC + c)
 
     barrier = pltpu.get_barrier_semaphore()
 
-    @pl.when(zh == 0)
-    def _():
-        pl.semaphore_signal(barrier, inc=1, device_id=at_h, device_id_type=MESH)
-
-    peers = [at_x(k, other) for k in (2, 1, 3, 0) for other in (False, True) if k or other]
-    for peer in peers:
-        pl.semaphore_signal(barrier, inc=1, device_id=peer, device_id_type=MESH)
+    everyone = [(k, other) for k in (2, 1, 3, 0) for other in (False, True)]
+    peers = [t for t in everyone if t != (0, False)]
+
+    def tell(device, sem=barrier):
+        pl.semaphore_signal(sem, inc=1, device_id=device, device_id_type=MESH)
+
+    @pl.when(lower)
+    def _():
+        tell(at_h)
+
+    @pl.when(jnp.logical_and(lower, zl >= NR + 1))
+    def _():
+        for t in peers:
+            tell(at_x(*t, half=1))
+
+    @pl.when(quick)
+    def _():
+        for z in (HUB, HUB + 1):
+            for i in range(NY):
+                tell((z * NY + i, ten))
+        tell(((HUB + 2 + side) * NY + y, ten))
+
+    @pl.when(hub)
+    def _():
+        tell(((HUB + 2 + side) * NY + y, ten))
+
+    @pl.when(last)
+    def _():
+        tell(((HUB + side) * NY + y, ten))
+
+    @pl.when(jnp.logical_or(hub, last))
+    def _():
+        for t in near:
+            tell(at_near(*t))
+
+    @pl.when(greets)
+    def _():
+        for t in peers:
+            tell(at_x(*t))
 
     @pl.when(reducer)
     def _():
-        for t in near:
-            pl.semaphore_signal(barrier, inc=1, device_id=at_near(*t), device_id_type=MESH)
-        for z in range(NR, NZ):
+        for z in range(NZ - NR - 1, -1, -1):
             for i in range(NY):
-                pl.semaphore_signal(barrier, inc=1, device_id=(z * NY + i, ten), device_id_type=MESH)
+                there = jnp.where(z < low, z, z + NR)
+                tell((there * NY + i, ten))
 
     def chunk(k, e):
         yy, ss = place(k, e)
@@ -80,16 +132,16 @@
         pltpu.make_async_copy(src, dst, load_sem.at[i])
         for i, (src, dst) in enumerate([(k_hbm, cot.at[c, zh, x]), (h_hbm, h), (w_hbm, w), (m_hbm, m), (v_hbm, v), (g_hbm, g), (o_hbm, o)])
     ]
-    for copy in loads:
-        copy.start()
-
     own = pltpu.make_async_copy(chunk(0, 0), raw.at[rep], load_sem.at[7])
 
-    @pl.when(reducer)
-    def _():
-        own.start()
-
-    pl.semaphore_wait(barrier, NY * NR - reducer.astype(jnp.int32) + len(peers) + zh)
+    waits = (
+        jnp.where(plain, NR * NY, 0)
+        + jnp.where(greets, len(peers), 0)
+        + jnp.where(upper, jnp.where(zl < NR + 1, 1, len(everyone)), 0)
+        + jnp.where(hub, len(near) + HUB * NY + 1, 0)
+        + jnp.where(last, len(near) + NZ // 2 - 1, 0)
+    )
+    pl.semaphore_wait(barrier, waits)
 
     def make(src, dst, sends, recvs, i, j, device):
         return pltpu.make_async_remote_copy(
@@ -100,75 +152,146 @@
     theirs = cot.at[c, 1 - zh, x]
     c_h = make(k_hbm, mine, send_c, recv_c, 0, 0, at_h)
     c_x = [make(k_hbm, mine, send_c, recv_c, k, k, at_x(k)) for k in (2, 1, 3)]
-    both = [(k, other) for k in (2, 1, 3, 0) for other in (False, True) if k or other]
-    c_hx = [make(theirs, theirs, send_c, recv_c, 4 + i, 4 + i, at_x(*t)) for i, t in enumerate(both)]
+    c_hx = [make(theirs, theirs, send_c, recv_c, 4 + i, 4 + i, at_x(*t)) for i, t in enumerate(peers)]
     row = cot.at[c, zh]
     c_c = make(row, row, send_c, recv_c, 11, 11, at_x(0, True))
 
-    @pl.when(zh == 1)
-    def _():
-        c_h.start()
-        pl.semaphore_signal(ready, inc=1, device_id=at_h, device_id_type=MESH)
-
     f_raw = [make(chunk(*t), raw.at[rep], send_r, recv_r, t[0] * NR + t[1], rep, at_near(*t)) for t in near]
     f_own = make(chunk(0, 0), raw.at[rep], send_r, recv_r, 0, rep, at_near(0, 0))
-    for copy in f_raw:
+
+    @pl.when(upper)
+    def _():
+        c_h.start()
+        tell(at_h, ready)
+
+    @pl.when(hub)
+    def _():
+        for z in range(0, HUB, NR):
+            tell(((z + side) * NY + y, ten), go)
+
+    @pl.when(jnp.logical_or(plain, jnp.logical_or(hub, last)))
+    def _():
+        for copy in f_raw:
+            copy.start()
+
+    @pl.when(plain)
+    def _():
+        f_own.start()
+
+    for copy in loads:
         copy.start()
 
-    @pl.when(jnp.logical_not(reducer))
-    def _():
-        f_own.start()
-
-    for copy in c_x:
+    @pl.when(upper)
+    def _():
+        own.start()
+        for copy in c_x:
+            copy.start()
+
+    @pl.when(quick)
+    def _():
+        pl.semaphore_wait(go, 1)
+        for copy in f_raw:
+            copy.start()
+
+    f_whole = [make(whole.at[me], whole.at[me], send_w, recv_w, t[0] * NR + t[1], t[0] * NR + t[1], at_near(*t)) for t in near]
+    f_z = [make(whole.at[me], whole.at[me], send_z, recv_z, z, side, at_z(z)) for z in range(NZ - NR)]
+
+    f_sum = [make(part, sums.at[pair], send_s, recv_s, k - 1, k - 1, at_pair(k)) for k in range(1, NZ // 2)]
+    f_direct = [make(whole.at[me], whole.at[me], send_d, recv_d, k, me, (lax.rem(y + k, NY), ten)) for k in (4, 3, 5, 2, 6, 1, 7, 0)]
+
+    def arrived(slot):
+        make(raw.at[slot], raw.at[slot], send_r, recv_r, 0, slot, at_y(1)).wait_recv()
+
+    @pl.when(reducer)
+    def _():
+        own.start()
+        arrived(first_plain * NY + y)
+        for copy in f_raw:
+            copy.start()
+        own.wait()
+
+        def plane(i, total):
+            z = jnp.where(i < 4, i + 3, jnp.where(i < 7, i - 4, 7))
+            for j in range(NY):
+                slot = z * NY + j
+
+                @pl.when(jnp.logical_and(slot != rep, slot != first_plain * NY + y))
+                def _():
+                    arrived(slot)
+
+            for j in range(NY):
+                total += raw[z * NY + j].astype(F32)
+            return total
+
+        whole[me] = lax.fori_loop(0, NZ, plane, jnp.zeros((16, 128), F32))
+        for copy in f_whole:
+            copy.start()
+
+        @pl.when(low == 0)
+        def _():
+            f_z[0].start()
+
+        @pl.when(low == 1)
+        def _():
+            for copy in f_direct:
+                copy.start()
+
+        for copy in f_z[1:]:
+            copy.start()
+
+    @pl.when(upper)
+    def _():
+        own.wait()
+        total = jnp.zeros((16, 128), F32)
+        for e in range(NR):
+            for j in range(NY):
+                slot = (low + e) * NY + j
+
+                @pl.when(slot != rep)
+                def _():
+                    arrived(slot)
+
+                total += raw[slot].astype(F32)
+        part[...] = total
+        for copy in f_sum:
+            copy.start()
+        sums[pair] = total
+
+    @pl.when(lower)
+    def _():
+        pl.semaphore_wait(ready, 1)
+        c_h.start()
+        for copy in c_x:
+            copy.start()
+
+    c_h.wait_recv()
+    for copy in c_hx:
         copy.start()
     loads[0].wait()
     for copy in c_x:
         copy.wait_recv()
     c_c.start()
 
-    f_whole = [make(whole.at[me], whole.at[me], send_w, recv_w, t[0] * NR + t[1], t[0] * NR + t[1], at_near(*t)) for t in near]
-    f_z = [make(whole.at[me], whole.at[me], send_z, recv_z, z, side, (z * NY + y, ten)) for z in range(NR, NZ)]
-
-    @pl.when(reducer)
-    def _():
-        own.wait()
-
-        def plane(z, total):
-            for i in range(NY):
-                slot = z * NY + i
-
-                @pl.when(slot != rep)
-                def _():
-                    make(raw.at[slot], raw.at[slot], send_r, recv_r, 0, slot, at_near(0, 1)).wait_recv()
-
-            for i in range(NY):
-                total += raw[z * NY + i].astype(F32)
-            return total
-
-        whole[me] = lax.fori_loop(0, NZ, plane, jnp.zeros((16, 128), F32))
-        for copy in f_whole:
-            copy.start()
-        for copy in f_z:
-            copy.start()
-
-    @pl.when(zh == 0)
-    def _():
-        pl.semaphore_wait(ready, 1)
-        c_h.start()
-
-    c_h.wait_recv()
-    for copy in c_hx:
-        copy.start()
-
     both_chunks = whole.at[pl.ds(y * NR, NR)]
     f_y = [make(both_chunks, both_chunks, send_y, recv_y, k, k, at_y(k)) for k in (4, 3, 5, 2, 6, 1, 7)]
 
-    @pl.when(jnp.logical_not(reducer))
+    @pl.when(column)
     def _():
         for i in range(NR):
             slot = whole.at[y * NR + i]
-            make(slot, slot, send_z, recv_z, 0, i, at_near(0, 0)).wait_recv()
+            make(slot, slot, send_z, recv_z, 0, i, at_y(1)).wait_recv()
         for copy in f_y:
+            copy.start()
+
+    @pl.when(upper)
+    def _():
+        for copy in f_sum:
+            copy.wait_recv()
+        total = sums[0]
+        for i in range(1, NZ // 2):
+            total += sums[i]
+        whole[me] = total
+        for copy in f_whole:
             copy.start()
 
     for copy in loads[1:5]:
@@ -182,24 +305,30 @@
         grad = lax.dot_general(h[:, rows], keys, (((0,), (0,)), ((), ())), preferred_element_type=F32)
         first = beta_one * m[rows].astype(F32) + (1.0 - beta_one) * grad
         second = beta_two * v[rows].astype(F32) + (1.0 - beta_two) * grad * grad
-        weight = w[rows].astype(F32)
-        update = first / corr_one / (jnp.sqrt(second / corr_two) + adam_eps) + decay_rate * weight
-        nw_ref[rows] = (weight - inner_rate * update).astype(BF16)
+        scaled = second * (1.0 / corr_two)
+        root = scaled * lax.rsqrt(scaled)
+        step = first * (inner_rate / corr_one) / (root + adam_eps)
+        nw_ref[rows] = (w[rows].astype(F32) * (1.0 - inner_rate * decay_rate) - step).astype(BF16)
         nm_ref[rows] = first.astype(BF16)
         nv_ref[rows] = second.astype(BF16)
 
     for copy in loads[5:]:
         copy.wait()
 
-    @pl.when(reducer)
+    @pl.when(inside)
     def _():
         for copy in f_whole:
             copy.wait_recv()
 
-    @pl.when(jnp.logical_not(reducer))
+    @pl.when(column)
     def _():
         for copy in f_y:
             copy.wait_recv()
+
+    @pl.when(direct)
+    def _():
+        for i in range(NR * NY):
+            make(whole.at[i], whole.at[i], send_d, recv_d, 0, i, at_y(1)).wait_recv()
 
     for i in range(NR * NY):
         r, q = (i // 4) * 16, (i % 4) * 128
@@ -212,14 +341,37 @@
     for copy in [c_h, c_c] + c_x + c_hx + f_raw:
         copy.wait_send()
 
+    @pl.when(inside)
+    def _():
+        for copy in f_whole:
+            copy.wait_send()
+
     @pl.when(reducer)
     def _():
-        for copy in f_whole + f_z:
+        for copy in f_z[1:]:
             copy.wait_send()
 
-    @pl.when(jnp.logical_not(reducer))
-    def _():
-        for copy in [f_own] + f_y:
+        @pl.when(low == 0)
+        def _():
+            f_z[0].wait_send()
+
+        @pl.when(low == 1)
+        def _():
+            for copy in f_direct:
+                copy.wait_send()
+
+    @pl.when(upper)
+    def _():
+        for copy in f_sum:
+            copy.wait_send()
+
+    @pl.when(plain)
+    def _():
+        f_own.wait_send()
+
+    @pl.when(column)
+    def _():
+        for copy in f_y:
             copy.wait_send()
 
 
@@ -257,6 +409,8 @@
             pltpu.VMEM((rows, kv), F32),
             pltpu.VMEM((NC, NH, NX, ktok, kv), BF16),
             pltpu.VMEM((NY * NZ, 16, 128), BF16),
+            pltpu.VMEM((16, 128), F32),
+            pltpu.VMEM((NZ // 2, 16, 128), F32),
             pltpu.VMEM((NR * NY, 16, 128), F32),
             pltpu.SemaphoreType.DMA((8,)),
             pltpu.SemaphoreType.DMA((12,)),
@@ -269,6 +423,11 @@
             pltpu.SemaphoreType.DMA((NR,)),
             pltpu.SemaphoreType.DMA((NY,)),
             pltpu.SemaphoreType.DMA((NY,)),
+            pltpu.SemaphoreType.DMA((3,)),
+            pltpu.SemaphoreType.DMA((3,)),
+            pltpu.SemaphoreType.DMA((NY,)),
+            pltpu.SemaphoreType.DMA((NR * NY,)),
+            pltpu.SemaphoreType.REGULAR,
             pltpu.SemaphoreType.REGULAR,
         ],
         compiler_params=pltpu.CompilerParams(

time: 37.9 us -> 34.9 us (0.921)
  Pallas kernels: 37.1 us -> 34.2 us
    pallas_call x1, Pallas kernels: 35.8 us -> 32.9 us  [per_device(): pl.pallas_call(kernel, out_shape=[jax.ShapeDtypeStruct((d, kv), BF16), ja...]
where the time goes in v4:
time: 34.9 us; the launch traced here: 34.8 us
  Pallas kernels  34.2 us (98%)
  between operations  0.64 us (2%)
    pallas_call x1, Pallas kernels, per_device(): pl.pallas_call(kernel, out_shape=[jax.ShapeDtypeStruct((d, kv), BF16), ja...  32.9 us
    pallas_call x1, Pallas kernels, per_device(): pl.pallas_call(store_kernel, out_shape=[jax.ShapeDtypeStruct(a.shape, a.d...  1.26 us

profile of v4, /device:TPU:1, one launch (start us, length us, event | category | flops | bytes accessed | tf_op | source)
XLA Modules:
  0.0 34.8 jit_solution(2838443974989904542)
XLA Ops:
  0.6 32.9 %shard_map.119 = (bf16[512,512]{1,0:T(8,128)(2,1)S(1)}, bf16[512,512]{1,0:T(8,128)(2,1)S(1)}, bf16[512,512]{1,0:T(8,128)(2,1)S(1)}, f32[64,512]{1,0:T(8,128)S(1)}, f32[64,512]{1,0:T(8,128)S(1)}) custom-call(bf16[256,512]{1,0:T(8,128)(2,1)} %bitcast.12, bf16[16,512]{1,0:T(8,128)(2,1)} %bitcast.14, bf16[512,512]{1,0:T(8,128)(2,1)} %bitcast.9, ...), custom_call_target="tpu_custom_call" | custom-call | tf_op jit(solution)/shard_map/pallas_call | solution.py:392
  33.5 1.3 %shard_map.120 = (bf16[512,512]{1,0:T(8,128)(2,1)}, bf16[512,512]{1,0:T(8,128)(2,1)}, bf16[512,512]{1,0:T(8,128)(2,1)}, f32[64,512]{1,0:T(8,128)}, f32[64,512]{1,0:T(8,128)}) custom-call(bf16[512,512]{1,0:T(8,128)(2,1)S(1)} %get-tuple-element.15.refs_0_, bf16[512,512]{1,0:T(8,128)(2,1)S(1)} %get-tuple-element.16.refs_1_, ...), custom_call_target="tpu_custom_call" | custom-call | tf_op jit(solution)/shard_map/pallas_call | solution.py:437

commit v5 on v4

--- a/solution.py
+++ b/solution.py
@@ -36,7 +36,11 @@
     upper = zh == 1
     lower = zh == 0
     pair = zl // 2
-    low = jnp.where(upper, pair * 2, jnp.where(ten == 0, 1, 0))
+
+    def low_of(yy):
+        return jnp.where(jnp.logical_and(ten == 0, yy == 0), 1, 0)
+
+    low = jnp.where(upper, pair * 2, low_of(y))
     side = zl - low
     inside = jnp.logical_and(side >= 0, side < NR)
     reducer = jnp.logical_and(lower, inside)
@@ -44,12 +48,17 @@
     direct = jnp.logical_and(lower, side < 0)
     column = jnp.logical_and(lower, side >= NR)
     side = lax.rem(zl + jnp.where(upper, 0, low), NR)
+    bridge = jnp.logical_and(reducer, zl == NR)
     me = y * NR + side
     quick = jnp.logical_and(upper, zl < HUB)
     hub = jnp.logical_and(upper, pair == HUB // 2)
     last = jnp.logical_and(upper, pair == HUB // 2 + 1)
     greets = jnp.logical_or(upper, zl < NR + 1)
     first_plain = 3
+    row = rep == 0
+    late = jnp.logical_and(row, ten == 0)
+    stand = jnp.logical_and(row, ten == 1)
+    far = jnp.logical_and(row, ten == NX * NC)
 
     near = sorted(((k, e) for k in range(NY) for e in range(NR) if k + e > 0), key=lambda t: -(min(t[0], NY - t[0]) + t[1]))
 
@@ -58,7 +67,7 @@
 
     def at_near(k, e):
         yy, ss = place(k, e)
-        return ((low + ss) * NY + yy, ten)
+        return ((jnp.where(upper, low, low_of(yy)) + ss) * NY + yy, ten)
 
     def at_y(k):
         return (zl * NY + lax.rem(y + k, NY), ten)
@@ -82,14 +91,13 @@
     def tell(device, sem=barrier):
         pl.semaphore_signal(sem, inc=1, device_id=device, device_id_type=MESH)
 
-    @pl.when(lower)
+    @pl.when(reducer)
     def _():
         tell(at_h)
 
-    @pl.when(jnp.logical_and(lower, zl >= NR + 1))
-    def _():
-        for t in peers:
-            tell(at_x(*t, half=1))
+    @pl.when(stand)
+    def _():
+        tell((rep, NX * NC))
 
     @pl.when(quick)
     def _():
@@ -120,7 +128,7 @@
     def _():
         for z in range(NZ - NR - 1, -1, -1):
             for i in range(NY):
-                there = jnp.where(z < low, z, z + NR)
+                there = jnp.where(z < low_of(i), z, z + NR)
                 tell((there * NY + i, ten))
 
     def chunk(k, e):
@@ -153,17 +161,27 @@
     c_h = make(k_hbm, mine, send_c, recv_c, 0, 0, at_h)
     c_x = [make(k_hbm, mine, send_c, recv_c, k, k, at_x(k)) for k in (2, 1, 3)]
     c_hx = [make(theirs, theirs, send_c, recv_c, 4 + i, 4 + i, at_x(*t)) for i, t in enumerate(peers)]
-    row = cot.at[c, zh]
-    c_c = make(row, row, send_c, recv_c, 11, 11, at_x(0, True))
+    half = cot.at[c, zh]
+    c_c = make(half, half, send_c, recv_c, 11, 11, at_x(0, True))
+    missed = cot.at[0, 1, 0]
+    c_far = make(k_hbm, missed, send_c, recv_c, 0, 12, (rep, 1))
+    c_stand = [
+        make(missed, missed, send_c, recv_c, 13 + i, 0 if t == (0, True) else 4 + i, (rep, 0 if t == (0, True) else t[0] * NC + t[1]))
+        for i, t in enumerate(peers)
+    ]
 
     f_raw = [make(chunk(*t), raw.at[rep], send_r, recv_r, t[0] * NR + t[1], rep, at_near(*t)) for t in near]
     f_own = make(chunk(0, 0), raw.at[rep], send_r, recv_r, 0, rep, at_near(0, 0))
 
-    @pl.when(upper)
+    @pl.when(jnp.logical_and(upper, jnp.logical_not(far)))
     def _():
         c_h.start()
         tell(at_h, ready)
 
+    @pl.when(far)
+    def _():
+        c_far.start()
+
     @pl.when(hub)
     def _():
         for z in range(0, HUB, NR):
@@ -178,12 +196,24 @@
     def _():
         f_own.start()
 
+    @pl.when(jnp.logical_and(plain, jnp.logical_not(late)))
+    def _():
+        tell(at_h)
+
+    @pl.when(jnp.logical_and(lower, zl >= NR + 1))
+    def _():
+        for t in peers:
+            tell(at_x(*t, half=1))
+
     for copy in loads:
         copy.start()
 
     @pl.when(upper)
     def _():
         own.start()
+
+    @pl.when(greets)
+    def _():
         for copy in c_x:
             copy.start()
 
@@ -197,7 +227,13 @@
     f_z = [make(whole.at[me], whole.at[me], send_z, recv_z, z, side, at_z(z)) for z in range(NZ - NR)]
 
     f_sum = [make(part, sums.at[pair], send_s, recv_s, k - 1, k - 1, at_pair(k)) for k in range(1, NZ // 2)]
-    f_direct = [make(whole.at[me], whole.at[me], send_d, recv_d, k, me, (lax.rem(y + k, NY), ten)) for k in (4, 3, 5, 2, 6, 1, 7, 0)]
+    f_direct = [make(whole.at[me], whole.at[me], send_d, recv_d, k, me, (0, 0)) for k in (0,)]
+
+    def own_half():
+        loads[0].wait()
+        for copy in c_x:
+            copy.wait_recv()
+        c_c.start()
 
     def arrived(slot):
         make(raw.at[slot], raw.at[slot], send_r, recv_r, 0, slot, at_y(1)).wait_recv()
@@ -208,6 +244,7 @@
         arrived(first_plain * NY + y)
         for copy in f_raw:
             copy.start()
+        own_half()
         own.wait()
 
         def plane(i, total):
@@ -224,19 +261,19 @@
             return total
 
         whole[me] = lax.fori_loop(0, NZ, plane, jnp.zeros((16, 128), F32))
-        for copy in f_whole:
+        for copy in f_whole[:7]:
             copy.start()
 
         @pl.when(low == 0)
         def _():
             f_z[0].start()
 
-        @pl.when(low == 1)
+        @pl.when(ten == 0)
         def _():
             for copy in f_direct:
                 copy.start()
 
-        for copy in f_z[1:]:
+        for copy in f_z[1:] + f_whole[7:]:
             copy.start()
 
     @pl.when(upper)
@@ -257,29 +294,64 @@
             copy.start()
         sums[pair] = total
 
-    @pl.when(lower)
+    @pl.when(jnp.logical_and(lower, jnp.logical_not(late)))
     def _():
         pl.semaphore_wait(ready, 1)
         c_h.start()
+
+    @pl.when(jnp.logical_not(greets))
+    def _():
         for copy in c_x:
             copy.start()
 
-    c_h.wait_recv()
-    for copy in c_hx:
-        copy.start()
-    loads[0].wait()
-    for copy in c_x:
-        copy.wait_recv()
-    c_c.start()
-
-    both_chunks = whole.at[pl.ds(y * NR, NR)]
-    f_y = [make(both_chunks, both_chunks, send_y, recv_y, k, k, at_y(k)) for k in (4, 3, 5, 2, 6, 1, 7)]
-
-    @pl.when(column)
-    def _():
+    chunks = whole.at[pl.ds(y * NR, NR)]
+    f_y = [make(chunks, chunks, send_y, recv_y, k, k, at_y(k)) for k in (4, 3, 5, 2, 6, 1, 7)]
+    f_skip = [jnp.logical_and(jnp.logical_and(ten == 0, zl == NR), lax.rem(y + k, NY) == 0) for k in (4, 3, 5, 2, 6, 1, 7)]
+
+    def along_y():
         for i in range(NR):
             slot = whole.at[y * NR + i]
             make(slot, slot, send_z, recv_z, 0, i, at_y(1)).wait_recv()
+        for skip, copy in zip(f_skip, f_y):
+
+            @pl.when(jnp.logical_not(skip))
+            def _():
+                copy.start()
+
+    @pl.when(jnp.logical_and(column, zl >= HUB))
+    def _():
+        along_y()
+
+    c_h.wait_recv()
+
+    @pl.when(late)
+    def _():
+        c_h.start()
+
+    @pl.when(jnp.logical_not(late))
+    def _():
+        for copy in c_hx:
+            copy.start()
+
+    @pl.when(stand)
+    def _():
+        c_far.wait_recv()
+        for copy in c_stand:
+            copy.start()
+
+    @pl.when(jnp.logical_and(column, zl < HUB))
+    def _():
+        along_y()
+
+    @pl.when(jnp.logical_not(reducer))
+    def _():
+        own_half()
+
+    f_next = f_whole[near.index((0, 1))]
+
+    @pl.when(bridge)
+    def _():
+        f_next.wait_recv()
         for copy in f_y:
             copy.start()
 
@@ -297,8 +369,15 @@
     for copy in loads[1:5]:
         copy.wait()
     c_c.wait_recv()
-    for copy in c_hx:
-        copy.wait_recv()
+    for t, copy in zip(peers, c_hx):
+        if t == (0, True):
+
+            @pl.when(jnp.logical_not(stand))
+            def _():
+                copy.wait_recv()
+
+        else:
+            copy.wait_recv()
     keys = jnp.concatenate([cot[k, i, j] for i in range(NH) for j in range(NX) for k in range(NC)], axis=0)
     for i in range(4):
         rows = slice(i * 128, i * 128 + 128)
@@ -312,13 +391,72 @@
         nm_ref[rows] = first.astype(BF16)
         nv_ref[rows] = second.astype(BF16)
 
+    for copy in [c_h, c_c] + c_x + f_raw:
+        copy.wait_send()
+
+    @pl.when(jnp.logical_not(late))
+    def _():
+        for copy in c_hx:
+            copy.wait_send()
+
+    @pl.when(stand)
+    def _():
+        for copy in c_stand:
+            copy.wait_send()
+
+    @pl.when(plain)
+    def _():
+        f_own.wait_send()
+
+    @pl.when(inside)
+    def _():
+        for copy in f_whole:
+            copy.wait_send()
+
+    @pl.when(reducer)
+    def _():
+        for copy in f_z[1:]:
+            copy.wait_send()
+
+        @pl.when(low == 0)
+        def _():
+            f_z[0].wait_send()
+
+        @pl.when(ten == 0)
+        def _():
+            for copy in f_direct:
+                copy.wait_send()
+
+    @pl.when(upper)
+    def _():
+        for copy in f_sum:
+            copy.wait_send()
+
+    @pl.when(column)
+    def _():
+        for skip, copy in zip(f_skip, f_y):
+
+            @pl.when(jnp.logical_not(skip))
+            def _():
+                copy.wait_send()
+
+    @pl.when(bridge)
+    def _():
+        for copy in f_y:
+            copy.wait_send()
+
     for copy in loads[5:]:
         copy.wait()
 
     @pl.when(inside)
     def _():
         for copy in f_whole:
-            copy.wait_recv()
+            if copy is not f_next:
+                copy.wait_recv()
+
+    @pl.when(jnp.logical_and(inside, jnp.logical_not(bridge)))
+    def _():
+        f_next.wait_recv()
 
     @pl.when(column)
     def _():
@@ -337,42 +475,6 @@
         fresh = outer_mu * o[area] + delta
         no_ref[area] = fresh
         ng_ref[area] = g[area] - outer_rate * (delta + outer_mu * fresh)
-
-    for copy in [c_h, c_c] + c_x + c_hx + f_raw:
-        copy.wait_send()
-
-    @pl.when(inside)
-    def _():
-        for copy in f_whole:
-            copy.wait_send()
-
-    @pl.when(reducer)
-    def _():
-        for copy in f_z[1:]:
-            copy.wait_send()
-
-        @pl.when(low == 0)
-        def _():
-            f_z[0].wait_send()
-
-        @pl.when(low == 1)
-        def _():
-            for copy in f_direct:
-                copy.wait_send()
-
-    @pl.when(upper)
-    def _():
-        for copy in f_sum:
-            copy.wait_send()
-
-    @pl.when(plain)
-    def _():
-        f_own.wait_send()
-
-    @pl.when(column)
-    def _():
-        for copy in f_y:
-            copy.wait_send()
 
 
 def store_kernel(*refs):
@@ -413,8 +515,8 @@
             pltpu.VMEM((NZ // 2, 16, 128), F32),
             pltpu.VMEM((NR * NY, 16, 128), F32),
             pltpu.SemaphoreType.DMA((8,)),
-            pltpu.SemaphoreType.DMA((12,)),
-            pltpu.SemaphoreType.DMA((12,)),
+            pltpu.SemaphoreType.DMA((20,)),
+            pltpu.SemaphoreType.DMA((13,)),
             pltpu.SemaphoreType.DMA((16,)),
             pltpu.SemaphoreType.DMA((NY * NZ,)),
             pltpu.SemaphoreType.DMA((16,)),
@@ -425,7 +527,7 @@
             pltpu.SemaphoreType.DMA((NY,)),
             pltpu.SemaphoreType.DMA((3,)),
             pltpu.SemaphoreType.DMA((3,)),
-            pltpu.SemaphoreType.DMA((NY,)),
+            pltpu.SemaphoreType.DMA((1,)),
             pltpu.SemaphoreType.DMA((NR * NY,)),
             pltpu.SemaphoreType.REGULAR,
             pltpu.SemaphoreType.REGULAR,

time: 34.9 us -> 33.6 us (0.963)
  Pallas kernels: 34.2 us -> 32.8 us
    pallas_call x1, Pallas kernels: 32.9 us -> 31.5 us  [per_device(): pl.pallas_call(kernel, out_shape=[jax.ShapeDtypeStruct((d, kv), BF16), ja...]
where the time goes in v5:
time: 33.6 us; the launch traced here: 33.4 us
  Pallas kernels  32.8 us (98%)
  between operations  0.64 us (2%)
    pallas_call x1, Pallas kernels, per_device(): pl.pallas_call(kernel, out_shape=[jax.ShapeDtypeStruct((d, kv), BF16), ja...  31.5 us
    pallas_call x1, Pallas kernels, per_device(): pl.pallas_call(store_kernel, out_shape=[jax.ShapeDtypeStruct(a.shape, a.d...  1.26 us

profile of v5, /device:TPU:1, one launch (start us, length us, event | category | flops | bytes accessed | tf_op | source)
XLA Modules:
  0.0 33.4 jit_solution(16806358149098993143)
XLA Ops:
  0.6 31.5 %shard_map.119 = (bf16[512,512]{1,0:T(8,128)(2,1)S(1)}, bf16[512,512]{1,0:T(8,128)(2,1)S(1)}, bf16[512,512]{1,0:T(8,128)(2,1)S(1)}, f32[64,512]{1,0:T(8,128)S(1)}, f32[64,512]{1,0:T(8,128)S(1)}) custom-call(bf16[256,512]{1,0:T(8,128)(2,1)} %bitcast.12, bf16[16,512]{1,0:T(8,128)(2,1)} %bitcast.14, bf16[512,512]{1,0:T(8,128)(2,1)} %bitcast.9, ...), custom_call_target="tpu_custom_call" | custom-call | tf_op jit(solution)/shard_map/pallas_call | solution.py:494
  32.2 1.3 %shard_map.120 = (bf16[512,512]{1,0:T(8,128)(2,1)}, bf16[512,512]{1,0:T(8,128)(2,1)}, bf16[512,512]{1,0:T(8,128)(2,1)}, f32[64,512]{1,0:T(8,128)}, f32[64,512]{1,0:T(8,128)}) custom-call(bf16[512,512]{1,0:T(8,128)(2,1)S(1)} %get-tuple-element.15.refs_0_, bf16[512,512]{1,0:T(8,128)(2,1)S(1)} %get-tuple-element.16.refs_1_, ...), custom_call_target="tpu_custom_call" | custom-call | tf_op jit(solution)/shard_map/pallas_call | solution.py:539

commit v6 on v5

--- a/solution.py
+++ b/solution.py
@@ -138,9 +138,9 @@
 
     loads = [
         pltpu.make_async_copy(src, dst, load_sem.at[i])
-        for i, (src, dst) in enumerate([(k_hbm, cot.at[c, zh, x]), (h_hbm, h), (w_hbm, w), (m_hbm, m), (v_hbm, v), (g_hbm, g), (o_hbm, o)])
+        for i, (src, dst) in enumerate([(k_hbm, cot.at[(c * NH + zh) * NX + x]), (h_hbm, h), (w_hbm, w), (m_hbm, m), (v_hbm, v), (g_hbm, g), (o_hbm, o)])
     ]
-    own = pltpu.make_async_copy(chunk(0, 0), raw.at[rep], load_sem.at[7])
+    own = pltpu.make_async_copy(chunk(0, 0), raw.at[rep], recv_r.at[zl])
 
     waits = (
         jnp.where(plain, NR * NY, 0)
@@ -156,22 +156,24 @@
             src_ref=src, dst_ref=dst, send_sem=sends.at[i], recv_sem=recvs.at[j], device_id=device, device_id_type=MESH
         )
 
-    mine = cot.at[c, zh, x]
-    theirs = cot.at[c, 1 - zh, x]
+    def blocks(n, i):
+        return make(cot.at[pl.ds(0, n)], cot.at[pl.ds(0, n)], send_c, recv_c, i, i, at_h)
+
+    mine = cot.at[(c * NH + zh) * NX + x]
+    theirs = cot.at[(c * NH + 1 - zh) * NX + x]
     c_h = make(k_hbm, mine, send_c, recv_c, 0, 0, at_h)
-    c_x = [make(k_hbm, mine, send_c, recv_c, k, k, at_x(k)) for k in (2, 1, 3)]
-    c_hx = [make(theirs, theirs, send_c, recv_c, 4 + i, 4 + i, at_x(*t)) for i, t in enumerate(peers)]
-    half = cot.at[c, zh]
-    c_c = make(half, half, send_c, recv_c, 11, 11, at_x(0, True))
-    missed = cot.at[0, 1, 0]
-    c_far = make(k_hbm, missed, send_c, recv_c, 0, 12, (rep, 1))
+    c_x = [make(k_hbm, mine, send_c, recv_c, 1, 1, at_x(k)) for k in (2, 1, 3)]
+    c_hx = [make(theirs, theirs, send_c, recv_c, 2, 2, at_x(*t)) for t in peers]
+    half = cot.at[pl.ds((c * NH + zh) * NX, NX)]
+    c_c = make(half, half, send_c, recv_c, 3, 3, at_x(0, True))
+    missed = cot.at[NX]
+    c_far = make(k_hbm, missed, send_c, recv_c, 0, 4, (rep, 1))
     c_stand = [
-        make(missed, missed, send_c, recv_c, 13 + i, 0 if t == (0, True) else 4 + i, (rep, 0 if t == (0, True) else t[0] * NC + t[1]))
-        for i, t in enumerate(peers)
+        make(missed, missed, send_c, recv_c, 4, 0 if t == (0, True) else 2, (rep, 0 if t == (0, True) else t[0] * NC + t[1])) for t in peers
     ]
 
-    f_raw = [make(chunk(*t), raw.at[rep], send_r, recv_r, t[0] * NR + t[1], rep, at_near(*t)) for t in near]
-    f_own = make(chunk(0, 0), raw.at[rep], send_r, recv_r, 0, rep, at_near(0, 0))
+    f_raw = [make(chunk(*t), raw.at[rep], send_r, recv_r, 0, zl, at_near(*t)) for t in near]
+    f_own = make(chunk(0, 0), raw.at[rep], send_r, recv_r, 1, zl, at_near(0, 0))
 
     @pl.when(jnp.logical_and(upper, jnp.logical_not(far)))
     def _():
@@ -223,38 +225,38 @@
         for copy in f_raw:
             copy.start()
 
-    f_whole = [make(whole.at[me], whole.at[me], send_w, recv_w, t[0] * NR + t[1], t[0] * NR + t[1], at_near(*t)) for t in near]
-    f_z = [make(whole.at[me], whole.at[me], send_z, recv_z, z, side, at_z(z)) for z in range(NZ - NR)]
-
-    f_sum = [make(part, sums.at[pair], send_s, recv_s, k - 1, k - 1, at_pair(k)) for k in range(1, NZ // 2)]
-    f_direct = [make(whole.at[me], whole.at[me], send_d, recv_d, k, me, (0, 0)) for k in (0,)]
+    f_whole = [make(whole.at[me], whole.at[me], send_w, recv_w, 0, int(t == (0, 1)), at_near(*t)) for t in near]
+    f_z = [make(whole.at[me], whole.at[me], send_z, recv_z, int(z > 0), 0, at_z(z)) for z in range(NZ - NR)]
+
+    f_sum = [make(part, sums.at[pair], send_s, recv_s, 0, 0, at_pair(k)) for k in range(1, NZ // 2)]
+    f_direct = [make(whole.at[me], whole.at[me], send_d, recv_d, 0, 0, (0, 0))]
 
     def own_half():
         loads[0].wait()
-        for copy in c_x:
-            copy.wait_recv()
+        blocks(NX - 1, 1).wait_recv()
         c_c.start()
 
-    def arrived(slot):
-        make(raw.at[slot], raw.at[slot], send_r, recv_r, 0, slot, at_y(1)).wait_recv()
+    def arrived(z):
+        there = raw.at[pl.ds(z * NY, NY)]
+        make(there, there, send_r, recv_r, 0, z, at_y(1)).wait_recv()
+
+    def sums_of(n, sends, recvs, i):
+        return make(whole.at[pl.ds(0, n)], whole.at[pl.ds(0, n)], sends, recvs, i, 0, at_y(1))
 
     @pl.when(reducer)
     def _():
         own.start()
-        arrived(first_plain * NY + y)
+        arrived(first_plain)
         for copy in f_raw:
             copy.start()
         own_half()
-        own.wait()
 
         def plane(i, total):
             z = jnp.where(i < 4, i + 3, jnp.where(i < 7, i - 4, 7))
-            for j in range(NY):
-                slot = z * NY + j
-
-                @pl.when(jnp.logical_and(slot != rep, slot != first_plain * NY + y))
-                def _():
-                    arrived(slot)
+
+            @pl.when(z != first_plain)
+            def _():
+                arrived(z)
 
             for j in range(NY):
                 total += raw[z * NY + j].astype(F32)
@@ -278,17 +280,11 @@
 
     @pl.when(upper)
     def _():
-        own.wait()
         total = jnp.zeros((16, 128), F32)
         for e in range(NR):
+            arrived(low + e)
             for j in range(NY):
-                slot = (low + e) * NY + j
-
-                @pl.when(slot != rep)
-                def _():
-                    arrived(slot)
-
-                total += raw[slot].astype(F32)
+                total += raw[(low + e) * NY + j].astype(F32)
         part[...] = total
         for copy in f_sum:
             copy.start()
@@ -305,13 +301,11 @@
             copy.start()
 
     chunks = whole.at[pl.ds(y * NR, NR)]
-    f_y = [make(chunks, chunks, send_y, recv_y, k, k, at_y(k)) for k in (4, 3, 5, 2, 6, 1, 7)]
+    f_y = [make(chunks, chunks, send_y, recv_y, 0, 0, at_y(k)) for k in (4, 3, 5, 2, 6, 1, 7)]
     f_skip = [jnp.logical_and(jnp.logical_and(ten == 0, zl == NR), lax.rem(y + k, NY) == 0) for k in (4, 3, 5, 2, 6, 1, 7)]
 
     def along_y():
-        for i in range(NR):
-            slot = whole.at[y * NR + i]
-            make(slot, slot, send_z, recv_z, 0, i, at_y(1)).wait_recv()
+        make(chunks, chunks, send_z, recv_z, 0, 0, at_y(1)).wait_recv()
         for skip, copy in zip(f_skip, f_y):
 
             @pl.when(jnp.logical_not(skip))
@@ -357,8 +351,8 @@
 
     @pl.when(upper)
     def _():
-        for copy in f_sum:
-            copy.wait_recv()
+        pairs = sums.at[pl.ds(0, NZ // 2 - 1)]
+        make(pairs, pairs, send_s, recv_s, 0, 0, at_y(1)).wait_recv()
         total = sums[0]
         for i in range(1, NZ // 2):
             total += sums[i]
@@ -369,16 +363,16 @@
     for copy in loads[1:5]:
         copy.wait()
     c_c.wait_recv()
-    for t, copy in zip(peers, c_hx):
-        if t == (0, True):
-
-            @pl.when(jnp.logical_not(stand))
-            def _():
-                copy.wait_recv()
-
-        else:
-            copy.wait_recv()
-    keys = jnp.concatenate([cot[k, i, j] for i in range(NH) for j in range(NX) for k in range(NC)], axis=0)
+
+    @pl.when(stand)
+    def _():
+        blocks(len(peers) - 1, 2).wait_recv()
+
+    @pl.when(jnp.logical_not(stand))
+    def _():
+        blocks(len(peers), 2).wait_recv()
+
+    keys = jnp.concatenate([cot[(k * NH + i) * NX + j] for i in range(NH) for j in range(NX) for k in range(NC)], axis=0)
     for i in range(4):
         rows = slice(i * 128, i * 128 + 128)
         grad = lax.dot_general(h[:, rows], keys, (((0,), (0,)), ((), ())), preferred_element_type=F32)
@@ -391,18 +385,19 @@
         nm_ref[rows] = first.astype(BF16)
         nv_ref[rows] = second.astype(BF16)
 
-    for copy in [c_h, c_c] + c_x + f_raw:
-        copy.wait_send()
+    c_h.wait_send()
+    c_c.wait_send()
+    blocks(NX - 1, 1).wait_send()
+    rest = raw.at[pl.ds(0, len(near))]
+    make(rest, rest, send_r, recv_r, 0, 0, at_y(1)).wait_send()
 
     @pl.when(jnp.logical_not(late))
     def _():
-        for copy in c_hx:
-            copy.wait_send()
+        blocks(len(peers), 2).wait_send()
 
     @pl.when(stand)
     def _():
-        for copy in c_stand:
-            copy.wait_send()
+        blocks(len(peers), 4).wait_send()
 
     @pl.when(plain)
     def _():
@@ -410,13 +405,11 @@
 
     @pl.when(inside)
     def _():
-        for copy in f_whole:
-            copy.wait_send()
+        sums_of(len(near), send_w, recv_w, 0).wait_send()
 
     @pl.when(reducer)
     def _():
-        for copy in f_z[1:]:
-            copy.wait_send()
+        sums_of(NZ - NR - 1, send_z, recv_z, 1).wait_send()
 
         @pl.when(low == 0)
         def _():
@@ -424,35 +417,29 @@
 
         @pl.when(ten == 0)
         def _():
-            for copy in f_direct:
-                copy.wait_send()
+            f_direct[0].wait_send()
 
     @pl.when(upper)
     def _():
-        for copy in f_sum:
-            copy.wait_send()
-
-    @pl.when(column)
-    def _():
-        for skip, copy in zip(f_skip, f_y):
-
-            @pl.when(jnp.logical_not(skip))
-            def _():
-                copy.wait_send()
-
-    @pl.when(bridge)
-    def _():
-        for copy in f_y:
-            copy.wait_send()
+        pairs = sums.at[pl.ds(0, NZ // 2 - 1)]
+        make(pairs, pairs, send_s, recv_s, 0, 0, at_y(1)).wait_send()
+
+    fewer = jnp.logical_and(column, jnp.logical_and(ten == 0, zl == NR))
+
+    @pl.when(fewer)
+    def _():
+        sums_of(NR * (NY - 2), send_y, recv_y, 0).wait_send()
+
+    @pl.when(jnp.logical_and(jnp.logical_or(column, bridge), jnp.logical_not(fewer)))
+    def _():
+        sums_of(NR * (NY - 1), send_y, recv_y, 0).wait_send()
 
     for copy in loads[5:]:
         copy.wait()
 
     @pl.when(inside)
     def _():
-        for copy in f_whole:
-            if copy is not f_next:
-                copy.wait_recv()
+        sums_of(len(near) - 1, send_w, recv_w, 0).wait_recv()
 
     @pl.when(jnp.logical_and(inside, jnp.logical_not(bridge)))
     def _():
@@ -460,13 +447,11 @@
 
     @pl.when(column)
     def _():
-        for copy in f_y:
-            copy.wait_recv()
+        sums_of(NR * (NY - 1), send_y, recv_y, 0).wait_recv()
 
     @pl.when(direct)
     def _():
-        for i in range(NR * NY):
-            make(whole.at[i], whole.at[i], send_d, recv_d, 0, i, at_y(1)).wait_recv()
+        sums_of(NR * NY, send_d, recv_d, 0).wait_recv()
 
     for i in range(NR * NY):
         r, q = (i // 4) * 16, (i % 4) * 128
@@ -509,26 +494,26 @@
             pltpu.VMEM((d, kv), BF16),
             pltpu.VMEM((rows, kv), F32),
             pltpu.VMEM((rows, kv), F32),
-            pltpu.VMEM((NC, NH, NX, ktok, kv), BF16),
+            pltpu.VMEM((NC * NH * NX, ktok, kv), BF16),
             pltpu.VMEM((NY * NZ, 16, 128), BF16),
             pltpu.VMEM((16, 128), F32),
             pltpu.VMEM((NZ // 2, 16, 128), F32),
             pltpu.VMEM((NR * NY, 16, 128), F32),
-            pltpu.SemaphoreType.DMA((8,)),
-            pltpu.SemaphoreType.DMA((20,)),
-            pltpu.SemaphoreType.DMA((13,)),
-            pltpu.SemaphoreType.DMA((16,)),
-            pltpu.SemaphoreType.DMA((NY * NZ,)),
-            pltpu.SemaphoreType.DMA((16,)),
-            pltpu.SemaphoreType.DMA((16,)),
+            pltpu.SemaphoreType.DMA((7,)),
+            pltpu.SemaphoreType.DMA((5,)),
+            pltpu.SemaphoreType.DMA((5,)),
+            pltpu.SemaphoreType.DMA((2,)),
             pltpu.SemaphoreType.DMA((NZ,)),
-            pltpu.SemaphoreType.DMA((NR,)),
-            pltpu.SemaphoreType.DMA((NY,)),
-            pltpu.SemaphoreType.DMA((NY,)),
-            pltpu.SemaphoreType.DMA((3,)),
-            pltpu.SemaphoreType.DMA((3,)),
-            pltpu.SemaphoreType.DMA((1,)),
-            pltpu.SemaphoreType.DMA((NR * NY,)),
+            pltpu.SemaphoreType.DMA((1,)),
+            pltpu.SemaphoreType.DMA((2,)),
+            pltpu.SemaphoreType.DMA((2,)),
+            pltpu.SemaphoreType.DMA((1,)),
+            pltpu.SemaphoreType.DMA((1,)),
+            pltpu.SemaphoreType.DMA((1,)),
+            pltpu.SemaphoreType.DMA((1,)),
+            pltpu.SemaphoreType.DMA((1,)),
+            pltpu.SemaphoreType.DMA((1,)),
+            pltpu.SemaphoreType.DMA((1,)),
             pltpu.SemaphoreType.REGULAR,
             pltpu.SemaphoreType.REGULAR,
         ],

time: 33.6 us -> 32 us (0.952)
  Pallas kernels: 32.8 us -> 31.2 us
    pallas_call x1, Pallas kernels: 31.5 us -> 29.9 us  [per_device(): pl.pallas_call(kernel, out_shape=[jax.ShapeDtypeStruct((d, kv), BF16), ja...]
where the time goes in v6:
time: 32 us; the launch traced here: 31.8 us
  Pallas kernels  31.2 us (98%)
  between operations  0.64 us (2%)
    pallas_call x1, Pallas kernels, per_device(): pl.pallas_call(kernel, out_shape=[jax.ShapeDtypeStruct((d, kv), BF16), ja...  29.9 us
    pallas_call x1, Pallas kernels, per_device(): pl.pallas_call(store_kernel, out_shape=[jax.ShapeDtypeStruct(a.shape, a.d...  1.26 us

profile of v6, /device:TPU:1, one launch (start us, length us, event | category | flops | bytes accessed | tf_op | source)
XLA Modules:
  0.0 31.8 jit_solution(10566908946778583880)
XLA Ops:
  0.6 29.9 %shard_map.119 = (bf16[512,512]{1,0:T(8,128)(2,1)S(1)}, bf16[512,512]{1,0:T(8,128)(2,1)S(1)}, bf16[512,512]{1,0:T(8,128)(2,1)S(1)}, f32[64,512]{1,0:T(8,128)S(1)}, f32[64,512]{1,0:T(8,128)S(1)}) custom-call(bf16[256,512]{1,0:T(8,128)(2,1)} %bitcast.12, bf16[16,512]{1,0:T(8,128)(2,1)} %bitcast.14, bf16[512,512]{1,0:T(8,128)(2,1)} %bitcast.9, ...), custom_call_target="tpu_custom_call" | custom-call | tf_op jit(solution)/shard_map/pallas_call | solution.py:479
  30.5 1.3 %shard_map.120 = (bf16[512,512]{1,0:T(8,128)(2,1)}, bf16[512,512]{1,0:T(8,128)(2,1)}, bf16[512,512]{1,0:T(8,128)(2,1)}, f32[64,512]{1,0:T(8,128)}, f32[64,512]{1,0:T(8,128)}) custom-call(bf16[512,512]{1,0:T(8,128)(2,1)S(1)} %get-tuple-element.15.refs_0_, bf16[512,512]{1,0:T(8,128)(2,1)S(1)} %get-tuple-element.16.refs_1_, ...), custom_call_target="tpu_custom_call" | custom-call | tf_op jit(solution)/shard_map/pallas_call | solution.py:524

commit v7 on v6

--- a/solution.py
+++ b/solution.py
@@ -27,7 +27,7 @@
 def kernel(
     h_hbm, k_hbm, w_hbm, m_hbm, v_hbm, l_hbm, g_hbm, o_hbm,
     nw_ref, nm_ref, nv_ref, ng_ref, no_ref,
-    h, w, m, v, g, o, cot, raw, part, sums, whole,
+    h, w, m, v, g, o, cot, raw, part, sums, whole, ht, wide_w, wide_m, wide_v,
     load_sem, send_c, recv_c, send_r, recv_r, send_w, recv_w, send_z, recv_z, send_y, recv_y, send_s, recv_s, send_d, recv_d, ready, go,
 ):
     rep, ten = lax.axis_index("replica"), lax.axis_index("tensor")
@@ -362,6 +362,15 @@
 
     for copy in loads[1:5]:
         copy.wait()
+    ht[...] = h[...].T
+
+    @pl.loop(0, 16)
+    def _(i):
+        rows = pl.ds(pl.multiple_of(i * 32, 32), 32)
+        wide_w[rows] = w[rows].astype(F32) * (1.0 - inner_rate * decay_rate)
+        wide_m[rows] = beta_one * m[rows].astype(F32)
+        wide_v[rows] = beta_two * v[rows].astype(F32)
+
     c_c.wait_recv()
 
     @pl.when(stand)
@@ -375,13 +384,13 @@
     keys = jnp.concatenate([cot[(k * NH + i) * NX + j] for i in range(NH) for j in range(NX) for k in range(NC)], axis=0)
     for i in range(4):
         rows = slice(i * 128, i * 128 + 128)
-        grad = lax.dot_general(h[:, rows], keys, (((0,), (0,)), ((), ())), preferred_element_type=F32)
-        first = beta_one * m[rows].astype(F32) + (1.0 - beta_one) * grad
-        second = beta_two * v[rows].astype(F32) + (1.0 - beta_two) * grad * grad
+        grad = jnp.dot(ht[rows], keys, preferred_element_type=F32)
+        first = wide_m[rows] + (1.0 - beta_one) * grad
+        second = wide_v[rows] + (1.0 - beta_two) * grad * grad
         scaled = second * (1.0 / corr_two)
         root = scaled * lax.rsqrt(scaled)
         step = first * (inner_rate / corr_one) / (root + adam_eps)
-        nw_ref[rows] = (w[rows].astype(F32) * (1.0 - inner_rate * decay_rate) - step).astype(BF16)
+        nw_ref[rows] = (wide_w[rows] - step).astype(BF16)
         nm_ref[rows] = first.astype(BF16)
         nv_ref[rows] = second.astype(BF16)
 
@@ -499,6 +508,10 @@
             pltpu.VMEM((16, 128), F32),
             pltpu.VMEM((NZ // 2, 16, 128), F32),
             pltpu.VMEM((NR * NY, 16, 128), F32),
+            pltpu.VMEM((d, tok), BF16),
+            pltpu.VMEM((d, kv), F32),
+            pltpu.VMEM((d, kv), F32),
+            pltpu.VMEM((d, kv), F32),
             pltpu.SemaphoreType.DMA((7,)),
             pltpu.SemaphoreType.DMA((5,)),
             pltpu.SemaphoreType.DMA((5,)),

time: 32 us -> 31.8 us (level)
  no operation moved by 1% of the time
where the time goes in v7:
time: 31.8 us; the launch traced here: 31.6 us
  Pallas kernels  31 us (97%)
  between operations  0.64 us (2%)
    pallas_call x1, Pallas kernels, per_device(): pl.pallas_call(kernel, out_shape=[jax.ShapeDtypeStruct((d, kv), BF16), ja...  29.7 us
    pallas_call x1, Pallas kernels, per_device(): pl.pallas_call(store_kernel, out_shape=[jax.ShapeDtypeStruct(a.shape, a.d...  1.26 us

profile of v7, /device:TPU:1, one launch (start us, length us, event | category | flops | bytes accessed | tf_op | source)
XLA Modules:
  0.0 31.6 jit_solution(9612163975510996049)
XLA Ops:
  0.6 29.7 %shard_map.119 = (bf16[512,512]{1,0:T(8,128)(2,1)S(1)}, bf16[512,512]{1,0:T(8,128)(2,1)S(1)}, bf16[512,512]{1,0:T(8,128)(2,1)S(1)}, f32[64,512]{1,0:T(8,128)S(1)}, f32[64,512]{1,0:T(8,128)S(1)}) custom-call(bf16[256,512]{1,0:T(8,128)(2,1)} %bitcast.12, bf16[16,512]{1,0:T(8,128)(2,1)} %bitcast.14, bf16[512,512]{1,0:T(8,128)(2,1)} %bitcast.9, ...), custom_call_target="tpu_custom_call" | custom-call | tf_op jit(solution)/shard_map/pallas_call | solution.py:488
  30.3 1.3 %shard_map.120 = (bf16[512,512]{1,0:T(8,128)(2,1)}, bf16[512,512]{1,0:T(8,128)(2,1)}, bf16[512,512]{1,0:T(8,128)(2,1)}, f32[64,512]{1,0:T(8,128)}, f32[64,512]{1,0:T(8,128)}) custom-call(bf16[512,512]{1,0:T(8,128)(2,1)S(1)} %get-tuple-element.15.refs_0_, bf16[512,512]{1,0:T(8,128)(2,1)S(1)} %get-tuple-element.16.refs_1_, ...), custom_call_target="tpu_custom_call" | custom-call | tf_op jit(solution)/shard_map/pallas_call | solution.py:537
